TPU v7x, 512 devices: a whole 4x8x8 slice. The times are simulated.
512 devices in a mesh: azim: 32 (over y, x), axial: 8 (over z_lo, core), radial: 2 (over z_hi).
Axes of the slice: x: 4, y: 8, z: 8 (z_hi: 2, z_lo: 4; z = z_hi * 4 + z_lo), core: 2. Of those that a mesh axis runs over, the one named last changes fastest.
Arguments:
- density: float32 [128, 64, 256], P('azim', 'axial', 'radial'), may hold values from 0.9 to 1.1
- momentum: float32 [3, 128, 64, 256], P(None, 'azim', 'axial', 'radial'), may hold values from -0.35 to 0.35
- energy: float32 [128, 64, 256], P('azim', 'axial', 'radial'), may hold values from 1.5 to 2.21, as said below
- wall_flags: int32 [32, 16], P('azim', 'axial'), may hold values 0 or 1
- body_motion: float32 [6], replicated, may hold values from -0.15 to 0.15
Outputs:
- density_change: float32 [128, 64, 256], P('azim', 'axial', 'radial')
- momentum_change: float32 [3, 128, 64, 256], P(None, 'azim', 'axial', 'radial')
- energy_change: float32 [128, 64, 256], P('azim', 'axial', 'radial')
- body_next: float32 [6], replicated
Inputs may be any that keep to these rules, and one draw needn't show every extreme that they name: At every point energy minus |momentum|^2 / (2 density) lies between 1.5 and 2.0.
All inputs are finite; a program needn't handle non-finite values. No bound on the sum of `wall_flags` on one device may be relied on, other than what follows from the above.
Results may differ from a plain program's by a relative error of at most 0.0003.
Values sent between devices are 32-bit elements; how exact they have to be, the bound alone decides.
A program may use at most 64 MiB of HBM per device.

v0:
```python
import math

import jax
import jax.numpy as jnp
import numpy as np
from jax import lax
from jax.sharding import PartitionSpec as P

heat_ratio = 1.4
radius_in = 1.0
radius_out = 3.0
store_length = 8.0
cfl_number = 0.05
body_gain = 30.0
body_mass = 0.5
inertia_diag = (1.0, 1.0, 0.25)
free_values = (1.0, 0.0, 0.0, 0.5, 1.0 / (1.4 * 0.4) + 0.125)
highest = lax.Precision.HIGHEST


def passed_along(block, axis, distance):
    devices = range(lax.axis_size(axis))
    route = [((i - distance) % len(devices), i) for i in devices]
    return lax.ppermute(block, axis, route)


def with_halo(cells, sides, width):
    for axis, dim in sides:
        count = lax.axis_size(axis)
        ends = count - 1
        head = lax.slice_in_dim(cells, 0, width, axis=dim)
        tail = lax.slice_in_dim(cells, cells.shape[dim] - width, cells.shape[dim], axis=dim)
        cells = jnp.concatenate(
            [
                lax.ppermute(tail, axis, [(i, (i + 1) % count) for i in range(ends)]),
                cells,
                lax.ppermute(head, axis, [((i + 1) % count, i) for i in range(ends)]),
            ],
            axis=dim,
        )
    return cells


def fr_tables():
    outer_point = np.sqrt(3.0 / 7.0 + 2.0 / 7.0 * np.sqrt(6.0 / 5.0))
    inner_point = np.sqrt(3.0 / 7.0 - 2.0 / 7.0 * np.sqrt(6.0 / 5.0))
    points = np.array([-outer_point, -inner_point, inner_point, outer_point])
    outer_weight = (18.0 - np.sqrt(30.0)) / 36.0
    inner_weight = (18.0 + np.sqrt(30.0)) / 36.0
    weights = np.array([outer_weight, inner_weight, inner_weight, outer_weight])
    bary_weights = np.array(
        [1.0 / np.prod([points[i] - points[j] for j in range(4) if j != i]) for i in range(4)]
    )
    derivative = np.zeros((4, 4))
    for i in range(4):
        for j in range(4):
            if i != j:
                derivative[i, j] = bary_weights[j] / bary_weights[i] / (points[i] - points[j])
        derivative[i, i] = -np.sum(derivative[i])

    def basis_at(location):
        return np.array(
            [
                np.prod(
                    [(location - points[j]) / (points[i] - points[j]) for j in range(4) if j != i]
                )
                for i in range(4)
            ]
        )

    at_lower = basis_at(-1.0)
    at_upper = basis_at(1.0)
    third_slope = 0.5 * (15.0 * points * points - 3.0)
    fourth_slope = 0.5 * (35.0 * points**3 - 15.0 * points)
    slope_left = 0.5 * (fourth_slope - third_slope)
    slope_right = 0.5 * (fourth_slope + third_slope)
    return (points, weights, derivative, at_lower, at_upper, slope_left, slope_right)


def coordinates(node_count, first_elem, spacing, points):
    element_count = node_count // 4
    offsets = jnp.tile(jnp.asarray((points + 1.0) / 2.0, jnp.float32), element_count)
    element = (first_elem + jnp.arange(node_count, dtype=jnp.int32) // 4).astype(jnp.float32)
    return ((element + offsets) * spacing, element * spacing, (element + 1.0) * spacing)


def pressure_of(conserved):
    kinetic = (
        conserved[1] * conserved[1] + conserved[2] * conserved[2] + conserved[3] * conserved[3]
    )
    return (heat_ratio - 1.0) * (conserved[4] - 0.5 * kinetic / conserved[0])


def normal_velocity(conserved, normal):
    return (
        conserved[1] * normal[0] + conserved[2] * normal[1] + conserved[3] * normal[2]
    ) / conserved[0]


def normal_flux(conserved, normal, grid_speed):
    pressure = pressure_of(conserved)
    vel_normal = normal_velocity(conserved, normal)
    relative = vel_normal - grid_speed
    return jnp.stack(
        [
            conserved[0] * relative,
            conserved[1] * relative + pressure * normal[0],
            conserved[2] * relative + pressure * normal[1],
            conserved[3] * relative + pressure * normal[2],
            conserved[4] * relative + pressure * vel_normal,
        ]
    )


def line_speed(conserved, normal):
    sound = jnp.sqrt(heat_ratio * pressure_of(conserved) / conserved[0])
    return jnp.abs(normal_velocity(conserved, normal)) + sound


def rusanov(minus_side, plus_side, speed_minus, speed_plus, normal, grid_speed, metric):
    wave_bound = jnp.maximum(speed_minus, speed_plus) + jnp.abs(grid_speed)
    average = 0.5 * (
        normal_flux(minus_side, normal, grid_speed) + normal_flux(plus_side, normal, grid_speed)
    )
    return metric * (average - 0.5 * wave_bound * (plus_side - minus_side))


def wall_flux(plus_side, normal, grid_speed, metric):
    pressure = pressure_of(plus_side)
    zero_part = jnp.zeros_like(pressure)
    return metric * jnp.stack(
        [
            zero_part,
            pressure * normal[0],
            pressure * normal[1],
            pressure * normal[2],
            pressure * grid_speed,
        ]
    )


def free_speed(normal_z):
    return 0.5 * jnp.abs(normal_z) + 1.0


def radial_grid(motion, angle_pos, axial_pos):
    cos_t = jnp.cos(angle_pos)
    sin_t = jnp.sin(angle_pos)
    return (
        motion[0] * cos_t + motion[1] * sin_t + axial_pos * (motion[4] * cos_t - motion[3] * sin_t)
    )


def azim_grid(motion, angle_pos, axial_pos, radius):
    cos_t = jnp.cos(angle_pos)
    sin_t = jnp.sin(angle_pos)
    return (
        -motion[0] * sin_t
        + motion[1] * cos_t
        + motion[5] * radius
        - axial_pos * (motion[4] * sin_t + motion[3] * cos_t)
    )


def axial_grid(motion, angle_pos, radius):
    return motion[2] + radius * (motion[3] * jnp.sin(angle_pos) - motion[4] * jnp.cos(angle_pos))


def rigid_update(motion, wall_loads):
    velocity = motion[:3]
    rates_now = motion[3:]
    inertia = jnp.asarray(inertia_diag, jnp.float32)
    ang_momentum = inertia * rates_now
    gyroscopic = jnp.stack(
        [
            rates_now[1] * ang_momentum[2] - rates_now[2] * ang_momentum[1],
            rates_now[2] * ang_momentum[0] - rates_now[0] * ang_momentum[2],
            rates_now[0] * ang_momentum[1] - rates_now[1] * ang_momentum[0],
        ]
    )
    zero_part = jnp.zeros_like(wall_loads[0])
    force_vec = jnp.stack([wall_loads[0], wall_loads[1], zero_part])
    torque = jnp.stack([wall_loads[2], wall_loads[3], zero_part])
    return jnp.concatenate(
        [
            velocity + body_gain * force_vec / body_mass,
            rates_now + body_gain * (torque - gyroscopic) / inertia,
        ]
    )


def frame_source(conserved, rates):
    zero_part = jnp.zeros_like(conserved[0])
    return jnp.stack(
        [
            zero_part,
            -(rates[1] * conserved[3] - rates[2] * conserved[2]),
            -(rates[2] * conserved[1] - rates[0] * conserved[3]),
            -(rates[0] * conserved[2] - rates[1] * conserved[1]),
            zero_part,
        ]
    )


def element_mix(matrix, values, direction):
    array_shape = values.shape
    if direction < values.ndim - 1:
        split_shape = (
            array_shape[:direction]
            + (array_shape[direction] // 4, 4)
            + array_shape[direction + 1 :]
        )
        patterns = {1: "jk,cekxr->cejxr", 2: "jk,caekr->caejr"}
        mixed_values = jnp.einsum(
            patterns[direction],
            jnp.asarray(matrix, jnp.float32),
            values.reshape(split_shape),
            precision=highest,
        )
        return mixed_values.reshape(array_shape)
    point_count = array_shape[direction]
    position = np.arange(point_count) % 4
    total_sum = jnp.zeros(array_shape, jnp.float32)
    for offset in range(-3, 4):
        target_slot = position + offset
        inside = (target_slot >= 0) & (target_slot < 4)
        factor = np.where(inside, matrix[position, np.clip(target_slot, 0, 3)], 0.0)
        if np.any(factor != 0.0):
            total_sum = total_sum + jnp.asarray(factor, jnp.float32) * jnp.roll(
                values, -offset, axis=direction
            )
    return total_sum


def cut_item(member, begin_at, end_at, direction):
    if isinstance(member, float) or member.shape[direction - 1] == 1:
        return member
    return lax.slice_in_dim(member, begin_at, end_at, axis=direction - 1)


def cut_geometry(geometry, begin_at, end_at, direction):
    normal, grid_speed, metric = geometry
    return (
        tuple((cut_item(member, begin_at, end_at, direction) for member in normal)),
        cut_item(grid_speed, begin_at, end_at, direction),
        cut_item(metric, begin_at, end_at, direction),
    )


def layer_flux(minus_side, plus_side, geometry):
    normal, grid_speed, metric = geometry
    return rusanov(
        minus_side[:5], plus_side[:5], minus_side[5], plus_side[5], normal, grid_speed, metric
    )


def free_layer(template, geometry):
    free_base = jnp.asarray(free_values, jnp.float32).reshape((5,) + (1,) * (template.ndim - 1))
    state_part = jnp.broadcast_to(free_base, (5,) + template.shape[1:])
    speed_part = jnp.broadcast_to(free_speed(geometry[0][2]), template.shape[1:])[None]
    return jnp.concatenate([state_part, speed_part], axis=0)


def make_faces(exchange_fn, low_end, high_end, low_wall):

    def face_fluxes(own_low, own_high, geo_low, geo_high):
        from_low, from_high = exchange_fn(own_low, own_high)
        minus_low = jnp.where(low_end, free_layer(own_low, geo_low), from_low)
        plus_high = jnp.where(high_end, free_layer(own_high, geo_high), from_high)
        hat_low = layer_flux(minus_low, own_low, geo_low)
        if low_wall:
            hat_low = jnp.where(
                low_end, wall_flux(own_low[:5], geo_low[0], geo_low[1], geo_low[2]), hat_low
            )
        hat_high = layer_flux(own_high, plus_high, geo_high)
        return (hat_low, hat_high)

    return face_fluxes


def direction_part(conserved, direction, tables, node_geo, low_geo, high_geo, face_fluxes):
    points, weights, derivative, at_lower, at_upper, slope_left, slope_right = tables
    node_count = conserved.shape[direction]
    all_rows = np.ones((4, 1))
    lower_rows = all_rows * at_lower[None, :]
    upper_rows = all_rows * at_upper[None, :]
    mean_rows = all_rows * (0.5 * weights)[None, :]
    tile_shape = [node_count] + [1] * (3 - direction)
    left_tile = jnp.asarray(np.tile(slope_left, node_count // 4).reshape(tile_shape), jnp.float32)
    right_tile = jnp.asarray(np.tile(slope_right, node_count // 4).reshape(tile_shape), jnp.float32)
    normal, grid_speed, metric = node_geo
    node_flux = metric * normal_flux(conserved, normal, grid_speed)
    line_speeds = line_speed(conserved, normal)[None]
    lower_trace = element_mix(lower_rows, conserved, direction)
    upper_trace = element_mix(upper_rows, conserved, direction)
    speed_mean = element_mix(mean_rows, line_speeds, direction)
    flux_diff = element_mix(derivative, node_flux, direction)
    flux_lower = element_mix(lower_rows, node_flux, direction)
    flux_upper = element_mix(upper_rows, node_flux, direction)
    lower_full = jnp.concatenate([lower_trace, speed_mean], axis=0)
    upper_full = jnp.concatenate([upper_trace, speed_mean], axis=0)
    inner_geo = cut_geometry(low_geo, 4, node_count, direction)
    hat_inner = layer_flux(
        lax.slice_in_dim(upper_full, 0, node_count - 4, axis=direction),
        lax.slice_in_dim(lower_full, 4, node_count, axis=direction),
        inner_geo,
    )
    hat_low, hat_high = face_fluxes(
        lax.slice_in_dim(lower_full, 0, 1, axis=direction),
        lax.slice_in_dim(upper_full, node_count - 1, node_count, axis=direction),
        cut_geometry(low_geo, 0, 1, direction),
        cut_geometry(high_geo, node_count - 1, node_count, direction),
    )
    hat_lower = jnp.concatenate([jnp.repeat(hat_low, 4, axis=direction), hat_inner], axis=direction)
    hat_upper = jnp.concatenate(
        [hat_inner, jnp.repeat(hat_high, 4, axis=direction)], axis=direction
    )
    return flux_diff + left_tile * (hat_lower - flux_lower) + right_tile * (hat_upper - flux_upper)


def on_device(density, momentum, energy, wall_flags, body_motion):
    tables = fr_tables()
    at_lower = jnp.asarray(tables[3], jnp.float32)
    weights = jnp.asarray(tables[1], jnp.float32)
    nodes_azim, nodes_axial, nodes_radial = density.shape
    azim_elems = nodes_azim // 4
    axial_elems = nodes_axial // 4
    radial_elems = nodes_radial // 4
    azim_devices = lax.axis_size("azim")
    axial_devices = lax.axis_size("axial")
    radial_devices = lax.axis_size("radial")
    azim_index = lax.axis_index("azim")
    axial_index = lax.axis_index("axial")
    radial_index = lax.axis_index("radial")
    step_azim = 2.0 * math.pi / (azim_elems * azim_devices)
    step_axial = store_length / (axial_elems * axial_devices)
    step_radial = (radius_out - radius_in) / (radial_elems * radial_devices)
    time_step = cfl_number * min(step_radial, step_axial, radius_in * step_azim)
    angle_node, angle_low, angle_high = coordinates(
        nodes_azim, azim_index * azim_elems, step_azim, tables[0]
    )
    axial_node = coordinates(nodes_axial, axial_index * axial_elems, step_axial, tables[0])[0]
    depth_node, depth_low, depth_high = coordinates(
        nodes_radial, radial_index * radial_elems, step_radial, tables[0]
    )
    radius_node = radius_in + depth_node
    radius_low = radius_in + depth_low
    radius_high = radius_in + depth_high
    conserved = jnp.concatenate([density[None], momentum, energy[None]], axis=0)
    wall_state = jnp.einsum("caxk,k->cax", conserved[..., :4], at_lower, precision=highest)
    wall_press = pressure_of(wall_state)
    flag_nodes = jnp.repeat(jnp.repeat(wall_flags.astype(jnp.float32), 4, axis=0), 4, axis=1)
    weight_azim = jnp.tile(weights, azim_elems) * (0.5 * step_azim)
    weight_axial = jnp.tile(weights, axial_elems) * (0.5 * step_axial)
    node_area = radius_in * weight_azim[:, None] * weight_axial[None, :]
    pushed = flag_nodes * wall_press * node_area
    cos_col = jnp.cos(angle_node)[:, None]
    sin_col = jnp.sin(angle_node)[:, None]
    axial_row = axial_node[None, :]
    wall_loads = jnp.stack(
        [
            -jnp.sum(pushed * cos_col),
            -jnp.sum(pushed * sin_col),
            jnp.sum(pushed * axial_row * sin_col),
            -jnp.sum(pushed * axial_row * cos_col),
        ]
    )
    wall_loads = jnp.where(radial_index == 0, wall_loads, jnp.zeros_like(wall_loads))
    totals = lax.psum(wall_loads, ("azim", "axial", "radial"))
    body_next = rigid_update(body_motion, totals)
    rates_next = body_next[3:]
    angle_col = angle_node[:, None, None]
    angle_low_col = angle_low[:, None, None]
    angle_high_col = angle_high[:, None, None]
    axial_mid = axial_node[None, :, None]
    radius_row = radius_node[None, None, :]

    def azim_geo(angle_pos):
        return (
            (-jnp.sin(angle_pos), jnp.cos(angle_pos), 0.0),
            azim_grid(body_next, angle_pos, axial_mid, radius_row),
            1.0,
        )

    def azim_fluxes(own_low, own_high, geo_low, geo_high):
        from_high = passed_along(own_low[:, 0], "azim", -1)[:, None]
        hat_high = layer_flux(own_high, from_high, geo_high)
        hat_low = passed_along(hat_high[:, 0], "azim", 1)[:, None]
        return (hat_low, hat_high)

    dg_azim = direction_part(
        conserved,
        1,
        tables,
        azim_geo(angle_col),
        azim_geo(angle_low_col),
        azim_geo(angle_high_col),
        azim_fluxes,
    )

    def axial_exchange(own_low, own_high):
        paired = jnp.stack([own_low[:, :, 0], own_high[:, :, 0]], axis=1)
        extended = with_halo(paired, (("axial", 1),), 1)
        return (extended[:, 0][:, :, None], extended[:, 3][:, :, None])

    axial_geo = ((0.0, 0.0, 1.0), axial_grid(body_next, angle_col, radius_row), 1.0)
    dg_axial = direction_part(
        conserved,
        2,
        tables,
        axial_geo,
        axial_geo,
        axial_geo,
        make_faces(axial_exchange, axial_index == 0, axial_index == axial_devices - 1, False),
    )

    def radial_exchange(own_low, own_high):
        paired = jnp.stack([own_low[..., 0], own_high[..., 0]], axis=1)
        extended = with_halo(paired, (("radial", 1),), 1)
        return (extended[:, 0][..., None], extended[:, 3][..., None])

    radial_normal = (jnp.cos(angle_col), jnp.sin(angle_col), 0.0)
    radial_speed = radial_grid(body_next, angle_col, axial_mid)
    dg_radial = direction_part(
        conserved,
        3,
        tables,
        (radial_normal, radial_speed, radius_row),
        (radial_normal, radial_speed, radius_low[None, None, :]),
        (radial_normal, radial_speed, radius_high[None, None, :]),
        make_faces(radial_exchange, radial_index == 0, radial_index == radial_devices - 1, True),
    )
    residual = (
        frame_source(conserved, rates_next)
        - (2.0 / step_radial * dg_radial + 2.0 / step_azim * dg_azim) / radius_row
        - 2.0 / step_axial * dg_axial
    )
    increment = time_step * residual
    return (increment[0], increment[1:4], increment[4], body_next)


def solution(mesh):
    return jax.shard_map(
        on_device,
        mesh=mesh,
        in_specs=(
            P("azim", "axial", "radial"),
            P(None, "azim", "axial", "radial"),
            P("azim", "axial", "radial"),
            P("azim", "axial"),
            P(),
        ),
        out_specs=(
            P("azim", "axial", "radial"),
            P(None, "azim", "axial", "radial"),
            P("azim", "axial", "radial"),
            P(),
        ),
        check_vma=False,
    )
```

profile of v0, /device:TPU:1, one launch (start us, length us, event | category | flops | bytes accessed | tf_op | source)
XLA Modules:
  0.0 344.0 jit_solution(11390198860813855004)
XLA Ops:
  5.2 1.8 fusion.29
  7.1 1.4 multiply_reduce_fusion.3
  10.4 1.4 fusion.165
  21.0 106.1 %psum.7 = f32[4]{0:T(128)S(1)} all-reduce(f32[4]{0:T(128)S(1)} %broadcast_select_fusion.2), channel_id=1, replica_groups=mesh['azim'=32,'axial'=8,'radial'=2] {'azim','axial','radial'}, use_global_device_ids=true, to_apply=%region_4.5 | all-reduce | flops 4 | bytes 32 | tf_op jit(solution)/shard_map/psum | solution.py:369
  130.0 2.0 multiply_add_fusion.16
  131.9 3.1 multiply_add_fusion.19
  141.2 1.4 fusion.53
  147.1 2.6 abs_add_fusion.1
  151.9 3.2 collective-permute-start.2
  158.1 3.1 collective-permute-start.4
  161.2 1.9 collective-permute-start.5
  172.5 1.4 maximum_multiply_fusion.5
  182.0 1.4 multiply_add_fusion.2
  183.4 1.5 copy.871
  185.7 1.5 copy.872
  187.2 2.0 add.1774
  190.3 2.1 multiply_add_fusion.3
  192.4 2.3 copy.862
  194.7 2.4 copy.863
  197.1 3.1 add.1764
  200.2 2.3 copy.913
  202.5 1.8 fusion.27
  204.3 3.9 %collective-permute-start = (f32[6,1,4,8]{3,2,0,1:T(4,128)}, f32[6,1,4,8]{3,2,0,1:T(4,128)}, u32[]{:S(2)}, u32[]{:S(2)}) collective-permute-start(f32[6,1,4,8]{3,2,0,1:T(4,128)} %bitcast.179), channel_id=1, source_target_pairs={{0,1},{2,3},{4,5},{6,7},{8,9},{10,11},{12,13},{14,15},{16,17},{18,... | collective-permute-start | bytes 2312 | tf_op jit(solution)/shard_map/ppermute | solution.py:35
  208.2 1.5 collective-permute-start.1
  210.3 1.6 fusion.42
  211.8 1.6 bitcast_dynamic-update-slice_fusion.3
  214.5 3.3 bitcast_dynamic-update-slice_fusion.6
  218.9 1.7 copy.955
  222.4 3.0 broadcast_multiply_fusion.2
  225.3 1.4 broadcast_multiply_fusion.1
  232.2 1.6 fusion.172
  233.8 1.6 fusion.173
  238.0 1.4 constant_dynamic-update-slice_fusion.29
  246.7 1.5 copy.1036
  249.2 1.5 copy.956
  250.6 1.5 copy.969
  252.3 1.5 copy.972
  253.8 2.3 copy.944
  257.0 1.4 constant_dynamic-update-slice_fusion.74
  263.4 2.4 copy.926
  265.8 2.5 copy.927
  273.9 1.5 constant_dynamic-update-slice_fusion.73
  283.0 3.4 %fusion.6 = f32[5,4,8,124]{2,1,3,0:T(4,128)} fusion(f32[5,4,8,128]{2,1,3,0:T(4,128)S(1)} %add.1774, f32[5,4,8,128]{2,1,3,0:T(4,128)S(1)} %copy-done, f32[5,4,8,124]{2,1,3,0:T(4,128)} %copy.926, f32[5,4,8,124]{2,1,3,0:T(4,128)} %copy.927, f32[4,8,124]{1,0,2:T(4,128)} %fusion.26, f32[124]{0:T(128)} %slice_bitcast_fusion.21), kind=kLoop, calls=%fused_computation.10 | loop fusion | flops 119040 | bytes 413168 | tf_op jit(solution)/shard_map/mul | solution.py:125
  286.5 2.4 copy.932
  288.8 1.5 copy.989
  290.3 1.5 copy.990
  292.0 1.6 copy.992
  294.1 2.3 copy.928
  299.5 1.6 constant_dynamic-update-slice_fusion.63
  301.1 1.6 constant_dynamic-update-slice_fusion.79
  302.6 1.5 constant_dynamic-update-slice_fusion.58
  305.6 1.6 constant_dynamic-update-slice_fusion.60
  307.2 1.5 constant_dynamic-update-slice_fusion.55
  308.7 1.5 constant_dynamic-update-slice_fusion.80
  310.2 1.5 constant_dynamic-update-slice_fusion.75
  313.7 1.5 copy.988
  315.1 1.5 copy.991
  316.7 2.0 constant_dynamic-update-slice_fusion.49
  321.0 2.0 constant_dynamic-update-slice_fusion.44
  324.7 2.4 collective-permute-start.3
  327.2 4.4 %multiply_add_fusion = f32[5,4,8,128]{2,1,3,0:T(4,128)} fusion(f32[5,4,8,128]{2,1,3,0:T(4,128)} %copy.991, f32[5,4,8,128]{2,1,3,0:T(4,128)} %copy.992, f32[5,4,8,128]{2,1,3,0:T(4,128)} %copy.990, f32[5,4,8,128]{2,1,3,0:T(4,128)} %copy.988, f32[5,4,8,128]{2,1,3,0:T(4,128)S(1)} %copy-done.3, f32[8]{0:T(128)S(1)} %copy-done.128, f32[8]{0:T(128)S(1)} %copy-done.127), kind=kLoop, calls=%fused_computation.6 | loop fusion | flops 122880 | bytes 491584 | tf_op jit(solution)/shard_map/add | solution.py:318
  331.6 1.8 copy.993
  333.8 3.2 fusion.1
  337.4 1.8 copy.973
  (480 shorter events, 97.9 us)
Async XLA Ops:
  2.0 137.1 %copy-start.87 = (f32[4]{0:T(128)}, f32[4]{0:T(128)S(1)}, u32[]{:S(2)}) copy-start(f32[4]{0:T(128)S(1)} %get-tuple-element.59) | copy-start | bytes 52
  2.0 137.1 %copy-start.90 = (f32[4]{0:T(128)}, f32[4]{0:T(128)S(1)}, u32[]{:S(2)}) copy-start(f32[4]{0:T(128)S(1)} %get-tuple-element.294) | copy-start | bytes 52
  2.0 142.2 %copy-start.83 = (f32[4]{0:T(128)}, f32[4]{0:T(128)S(1)}, u32[]{:S(2)}) copy-start(f32[4]{0:T(128)S(1)} %get-tuple-element.293) | copy-start | bytes 52
  7.0 135.6 %copy-start.76 = (f32[8]{0:T(128)}, f32[8]{0:T(128)S(1)}, u32[]{:S(2)}) copy-start(f32[8]{0:T(128)S(1)} %get-tuple-element.288) | copy-start | bytes 100
  128.0 11.0 %copy-start.101 = (f32[3]{0:T(128)}, f32[3]{0:T(128)S(1)}, u32[]{:S(2)}) copy-start(f32[3]{0:T(128)S(1)} %get-tuple-element.284) | copy-start | bytes 40
  128.0 11.0 %copy-start.102 = (f32[3]{0:T(128)}, f32[3]{0:T(128)S(1)}, u32[]{:S(2)}) copy-start(f32[3]{0:T(128)S(1)} %get-tuple-element.285) | copy-start | bytes 40
  135.0 6.2 %copy-start.66 = (f32[4]{0:T(128)}, f32[4]{0:T(128)S(1)}, u32[]{:S(2)}) copy-start(f32[4]{0:T(128)S(1)} %get-tuple-element.251) | copy-start | bytes 52
  135.0 7.6 %copy-start.72 = (f32[4]{0:T(128)}, f32[4]{0:T(128)S(1)}, u32[]{:S(2)}) copy-start(f32[4]{0:T(128)S(1)} %get-tuple-element.252) | copy-start | bytes 52
  135.0 7.6 %copy-start.74 = (f32[4]{0:T(128)}, f32[4]{0:T(128)S(1)}, u32[]{:S(2)}) copy-start(f32[4]{0:T(128)S(1)} %get-tuple-element.253) | copy-start | bytes 52
  147.1 8.2 %copy-start.19 = (f32[3,4,8,128]{3,2,1,0:T(8,128)S(1)}, f32[3,4,8,128]{3,2,1,0:T(8,128)}, u32[]{:S(2)}) copy-start(f32[3,4,8,128]{3,2,1,0:T(8,128)} %param.76) | copy-start | bytes 147460
  147.1 8.2 %copy-start.48 = (f32[4,8,128]{2,1,0:T(8,128)S(1)}, f32[4,8,128]{2,1,0:T(8,128)}, u32[]{:S(2)}) copy-start(f32[4,8,128]{2,1,0:T(8,128)} %param.77) | copy-start | bytes 49156
  149.8 7.5 %copy-start.107 = (f32[4,4,1,1]{1,0,3,2:T(4,128)S(1)}, f32[4,4,1,1]{1,0,3,2:T(4,128)}, u32[]{:S(2)}) copy-start(f32[4,4,1,1]{1,0,3,2:T(4,128)} %constant.321) | copy-start | bytes 196
  151.0 12.9 %copy-start.63 = (f32[8,128,4]{1,0,2:T(8,128)}, f32[8,128,4]{1,0,2:T(8,128)S(1)}, u32[]{:S(2)}) copy-start(f32[8,128,4]{1,0,2:T(8,128)S(1)} %copy.1037) | copy-start | bytes 49156
  151.9 164.7 %collective-permute-start.2 = (f32[6,8,128]{2,1,0:T(8,128)}, f32[6,8,128]{2,1,0:T(8,128)}, u32[]{:S(2)}, u32[]{:S(2)}) collective-permute-start(f32[6,8,128]{2,1,0:T(8,128)} %fusion.49), channel_id=1, source_target_pairs={{16,0},{32,16},{48,32},{64,48},{80,64},{96,80},{112,96},{128,112},... | collective-permute-start | bytes 73736 | tf_op jit(solution)/shard_map/ppermute | solution.py:24
  156.3 6.9 %copy-start.16 = (f32[5,4,2,128,4]{3,4,2,1,0:T(4,128)}, f32[5,4,2,128,4]{3,4,2,1,0:T(4,128)S(1)}, u32[]{:S(2)}) copy-start(f32[5,4,2,128,4]{3,4,2,1,0:T(4,128)S(1)} %fusion.48) | copy-start | bytes 245764
  157.3 5.9 %copy-start.17 = (f32[5,4,2,128,4]{3,4,2,1,0:T(4,128)}, f32[5,4,2,128,4]{3,4,2,1,0:T(4,128)S(1)}, u32[]{:S(2)}) copy-start(f32[5,4,2,128,4]{3,4,2,1,0:T(4,128)S(1)} %fusion.47) | copy-start | bytes 245764
  157.5 5.7 %copy-start.56 = (f32[4,2,128,4]{2,3,1,0:T(4,128)}, f32[4,2,128,4]{2,3,1,0:T(4,128)S(1)}, u32[]{:S(2)}) copy-start(f32[4,2,128,4]{2,3,1,0:T(4,128)S(1)} %fusion.171) | copy-start | bytes 49156
  158.1 140.5 %collective-permute-start.4 = (f32[6,1,4,128]{3,2,0,1:T(4,128)}, f32[6,1,4,128]{3,2,0,1:T(4,128)}, u32[]{:S(2)}, u32[]{:S(2)}) collective-permute-start(f32[6,1,4,128]{3,2,0,1:T(4,128)} %bitcast.133), channel_id=1, source_target_pairs={{0,2},{2,4},{4,6},{6,8},{8,10},{10,12},{12,14},{1,3},{3,5},{5,7},{... | collective-permute-start | bytes 36872 | tf_op jit(solution)/shard_map/ppermute | solution.py:35
  161.2 137.4 %collective-permute-start.5 = (f32[6,1,4,128]{3,2,0,1:T(4,128)}, f32[6,1,4,128]{3,2,0,1:T(4,128)}, u32[]{:S(2)}, u32[]{:S(2)}) collective-permute-start(f32[6,1,4,128]{3,2,0,1:T(4,128)} %bitcast.150), channel_id=1, source_target_pairs={{2,0},{4,2},{6,4},{8,6},{10,8},{12,10},{14,12},{3,1},{5,3},{7,5},{... | collective-permute-start | bytes 36872 | tf_op jit(solution)/shard_map/ppermute | solution.py:37
  165.4 7.0 %copy-start.131 = (f32[128]{0:T(128)S(1)}, f32[128]{0:T(128)}, u32[]{:S(2)}) copy-start(f32[128]{0:T(128)} %constant.285.clone) | copy-start | bytes 1540
  168.0 8.1 %copy-start.15 = (f32[4,8,126]{1,0,2:T(4,128)S(1)}, f32[4,8,126]{1,0,2:T(4,128)}, u32[]{:S(2)}) copy-start(f32[4,8,126]{1,0,2:T(4,128)} %get-tuple-element.154) | copy-start | bytes 48388
  169.5 8.8 %copy-start.96 = (f32[4,8,2]{1,0,2:T(4,128)S(1)}, f32[4,8,2]{1,0,2:T(4,128)}, u32[]{:S(2)}) copy-start(f32[4,8,2]{1,0,2:T(4,128)} %get-tuple-element.156) | copy-start | bytes 772
  176.3 5.7 %copy-start.22 = (f32[5,4,8,3]{3,2,1,0:T(8,128)S(1)}, f32[5,4,8,3]{3,2,1,0:T(8,128)}, u32[]{:S(2)}) copy-start(f32[5,4,8,3]{3,2,1,0:T(8,128)} %get-tuple-element.178) | copy-start | bytes 5764
  176.3 5.7 %copy-start.24 = (f32[4,8,128]{2,1,0:T(8,128)S(1)}, f32[4,8,128]{2,1,0:T(8,128)}, u32[]{:S(2)}) copy-start(f32[4,8,128]{2,1,0:T(8,128)} %param.75) | copy-start | bytes 49156
  202.5 10.9 %copy-start.53 = (f32[4,8]{1,0:T(4,128)S(1)}, f32[4,8]{1,0:T(4,128)}, u32[]{:S(2)}) copy-start(f32[4,8]{1,0:T(4,128)} %copy-done.52) | copy-start | bytes 388
  202.5 10.9 %copy-start.65 = (f32[4,8]{1,0:T(4,128)S(1)}, f32[4,8]{1,0:T(4,128)}, u32[]{:S(2)}) copy-start(f32[4,8]{1,0:T(4,128)} %copy-done.64) | copy-start | bytes 388
  202.5 10.9 %copy-start.84 = (f32[4]{0:T(128)S(1)}, f32[4]{0:T(128)}, u32[]{:S(2)}) copy-start(f32[4]{0:T(128)} %copy-done.83) | copy-start | bytes 52
  202.5 10.9 %copy-start.93 = (f32[4]{0:T(128)S(1)}, f32[4]{0:T(128)}, u32[]{:S(2)}) copy-start(f32[4]{0:T(128)} %get-tuple-element.275) | copy-start | bytes 52
  204.3 92.1 %collective-permute-start = (f32[6,1,4,8]{3,2,0,1:T(4,128)}, f32[6,1,4,8]{3,2,0,1:T(4,128)}, u32[]{:S(2)}, u32[]{:S(2)}) collective-permute-start(f32[6,1,4,8]{3,2,0,1:T(4,128)} %bitcast.179), channel_id=1, source_target_pairs={{0,1},{2,3},{4,5},{6,7},{8,9},{10,11},{12,13},{14,15},{16,17},{18,... | collective-permute-start | bytes 2312 | tf_op jit(solution)/shard_map/ppermute | solution.py:35
  208.2 88.2 %collective-permute-start.1 = (f32[6,1,4,8]{3,2,0,1:T(4,128)}, f32[6,1,4,8]{3,2,0,1:T(4,128)}, u32[]{:S(2)}, u32[]{:S(2)}) collective-permute-start(f32[6,1,4,8]{3,2,0,1:T(4,128)} %bitcast.180), channel_id=1, source_target_pairs={{1,0},{3,2},{5,4},{7,6},{9,8},{11,10},{13,12},{15,14},{17,16},{19,... | collective-permute-start | bytes 2312 | tf_op jit(solution)/shard_map/ppermute | solution.py:37
  230.1 6.7 %copy-start.7 = (f32[4,128]{0,1:T(8,128)S(1)}, f32[4,128]{0,1:T(8,128)}, u32[]{:S(2)}) copy-start(f32[4,128]{0,1:T(8,128)} %copy-done.6) | copy-start | bytes 6148
  230.1 7.8 %copy-start.4 = (f32[5,4,8,128]{3,2,1,0:T(8,128)S(1)}, f32[5,4,8,128]{3,2,1,0:T(8,128)}, u32[]{:S(2)}) copy-start(f32[5,4,8,128]{3,2,1,0:T(8,128)} %copy.897) | copy-start | bytes 245764
  230.1 7.8 %copy-start.5 = (f32[5,4,8,128]{3,2,1,0:T(8,128)S(1)}, f32[5,4,8,128]{3,2,1,0:T(8,128)}, u32[]{:S(2)}) copy-start(f32[5,4,8,128]{3,2,1,0:T(8,128)} %copy.913) | copy-start | bytes 245764
  230.1 7.8 %copy-start.54 = (f32[4,8]{1,0:T(4,128)S(1)}, f32[4,8]{1,0:T(4,128)}, u32[]{:S(2)}) copy-start(f32[4,8]{1,0:T(4,128)} %copy-done.52) | copy-start | bytes 388
  230.1 7.8 %copy-start.88 = (f32[4]{0:T(128)S(1)}, f32[4]{0:T(128)}, u32[]{:S(2)}) copy-start(f32[4]{0:T(128)} %copy-done.87) | copy-start | bytes 52
  230.8 10.3 %copy-start.51 = (f32[4,128]{0,1:T(8,128)S(1)}, f32[4,128]{0,1:T(8,128)}, u32[]{:S(2)}) copy-start(f32[4,128]{0,1:T(8,128)} %get-tuple-element.271) | copy-start | bytes 6148
  232.2 18.5 %copy-start.42 = (f32[5,8,128,4]{2,3,1,0:T(4,128)S(1)}, f32[5,8,128,4]{2,3,1,0:T(4,128)}, u32[]{:S(2)}) copy-start(f32[5,8,128,4]{2,3,1,0:T(4,128)} %fusion.168) | copy-start | bytes 245764
  236.8 20.2 %copy-start.69 = (f32[4,128]{1,0:T(4,128)}, f32[4,128]{1,0:T(4,128)S(1)}, u32[]{:S(2)}) copy-start(f32[4,128]{1,0:T(4,128)S(1)} %copy.986) | copy-start | bytes 6148
  252.2 6.2 %copy-start.50 = (f32[4,128]{0,1:T(8,128)S(1)}, f32[4,128]{0,1:T(8,128)}, u32[]{:S(2)}) copy-start(f32[4,128]{0,1:T(8,128)} %get-tuple-element.267) | copy-start | bytes 6148
  252.2 6.3 %copy-start.57 = (f32[4,2,128,4]{2,3,1,0:T(4,128)S(1)}, f32[4,2,128,4]{2,3,1,0:T(4,128)}, u32[]{:S(2)}) copy-start(f32[4,2,128,4]{2,3,1,0:T(4,128)} %copy-done.56) | copy-start | bytes 49156
  252.2 6.9 %copy-start = (f32[5,4,8,128]{2,1,3,0:T(4,128)S(1)}, f32[5,4,8,128]{2,1,3,0:T(4,128)}, u32[]{:S(2)}) copy-start(f32[5,4,8,128]{2,1,3,0:T(4,128)} %add.1764) | copy-start | bytes 245764
  252.2 6.9 %copy-start.73 = (f32[4]{0:T(128)S(1)}, f32[4]{0:T(128)}, u32[]{:S(2)}) copy-start(f32[4]{0:T(128)} %copy-done.72) | copy-start | bytes 52
  252.2 6.9 %copy-start.75 = (f32[4]{0:T(128)S(1)}, f32[4]{0:T(128)}, u32[]{:S(2)}) copy-start(f32[4]{0:T(128)} %copy-done.74) | copy-start | bytes 52
  252.2 6.9 %copy-start.77 = (f32[8]{0:T(128)S(1)}, f32[8]{0:T(128)}, u32[]{:S(2)}) copy-start(f32[8]{0:T(128)} %copy-done.76) | copy-start | bytes 100
  252.2 6.9 %copy-start.85 = (f32[4]{0:T(128)S(1)}, f32[4]{0:T(128)}, u32[]{:S(2)}) copy-start(f32[4]{0:T(128)} %copy-done.83) | copy-start | bytes 52
  252.2 6.9 %copy-start.91 = (f32[4]{0:T(128)S(1)}, f32[4]{0:T(128)}, u32[]{:S(2)}) copy-start(f32[4]{0:T(128)} %copy-done.90) | copy-start | bytes 52
  252.2 7.5 %copy-start.100 = (f32[4,8]{1,0:T(4,128)S(1)}, f32[4,8]{1,0:T(4,128)}, u32[]{:S(2)}) copy-start(f32[4,8]{1,0:T(4,128)} %get-tuple-element.246) | copy-start | bytes 388
  253.8 6.8 %copy-start.55 = (f32[4,8]{1,0:T(4,128)S(1)}, f32[4,8]{1,0:T(4,128)}, u32[]{:S(2)}) copy-start(f32[4,8]{1,0:T(4,128)} %copy-done.52) | copy-start | bytes 388
  253.8 7.5 %copy-start.94 = (f32[4]{0:T(128)S(1)}, f32[4]{0:T(128)}, u32[]{:S(2)}) copy-start(f32[4]{0:T(128)} %get-tuple-element.275) | copy-start | bytes 52
  263.4 6.6 %copy-start.14 = (f32[1,4,8,128]{2,1,3,0:T(4,128)S(1)}, f32[1,4,8,128]{2,1,3,0:T(4,128)}, u32[]{:S(2)}) copy-start(f32[1,4,8,128]{2,1,3,0:T(4,128)} %get-tuple-element.135) | copy-start | bytes 49156
  263.4 7.3 %copy-start.13 = (f32[1,4,8,128]{2,1,3,0:T(4,128)S(1)}, f32[1,4,8,128]{2,1,3,0:T(4,128)}, u32[]{:S(2)}) copy-start(f32[1,4,8,128]{2,1,3,0:T(4,128)} %get-tuple-element.136) | copy-start | bytes 49156
  265.8 8.1 %copy-start.70 = (f32[4,128]{1,0:T(4,128)S(1)}, f32[4,128]{1,0:T(4,128)}, u32[]{:S(2)}) copy-start(f32[4,128]{1,0:T(4,128)} %copy-done.69) | copy-start | bytes 6148
  291.9 6.0 %copy-start.134 = (f32[1,1,128]{2,1,0:T(1,128)S(1)}, f32[1,1,128]{2,1,0:T(1,128)}, u32[]{:S(2)}) copy-start(f32[1,1,128]{2,1,0:T(1,128)} %get-tuple-element.306) | copy-start | bytes 1540
  291.9 6.7 %copy-start.129 = (f32[6]{0:T(128)S(1)}, f32[6]{0:T(128)}, u32[]{:S(2)}) copy-start(f32[6]{0:T(128)} %constant.312) | copy-start | bytes 76
  291.9 7.5 %copy-start.62 = (f32[128]{0:T(128)S(1)}, f32[128]{0:T(128)}, u32[]{:S(2)}) copy-start(f32[128]{0:T(128)} %copy-done.59) | copy-start | bytes 1540
  291.9 7.5 %copy-start.68 = (f32[4]{0:T(128)S(1)}, f32[4]{0:T(128)}, u32[]{:S(2)}) copy-start(f32[4]{0:T(128)} %copy-done.66) | copy-start | bytes 52
  292.0 7.5 %copy-start.82 = (f32[1,4,1,128]{3,2,1,0:T(1,128)S(1)}, f32[1,4,1,128]{3,2,1,0:T(1,128)}, u32[]{:S(2)}) copy-start(f32[1,4,1,128]{3,2,1,0:T(1,128)} %get-tuple-element.65) | copy-start | bytes 6148
  292.0 7.5 %copy-start.99 = (f32[5,4,1,128]{3,2,1,0:T(1,128)S(1)}, f32[5,4,1,128]{3,2,1,0:T(1,128)}, u32[]{:S(2)}) copy-start(f32[5,4,1,128]{3,2,1,0:T(1,128)} %get-tuple-element.64) | copy-start | bytes 30724
  313.6 7.3 %copy-start.47 = (f32[5,8,128,4]{2,1,3,0:T(8,128)S(1)}, f32[5,8,128,4]{2,1,3,0:T(8,128)}, u32[]{:S(2)}) copy-start(f32[5,8,128,4]{2,1,3,0:T(8,128)} %copy.1036) | copy-start | bytes 245764
  313.6 13.5 %copy-start.3 = (f32[5,4,8,128]{2,1,3,0:T(4,128)S(1)}, f32[5,4,8,128]{2,1,3,0:T(4,128)}, u32[]{:S(2)}) copy-start(f32[5,4,8,128]{2,1,3,0:T(4,128)} %copy.989) | copy-start | bytes 245764
  313.6 13.5 %copy-start.127 = (f32[8]{0:T(128)S(1)}, f32[8]{0:T(128)}, u32[]{:S(2)}) copy-start(f32[8]{0:T(128)} %constant.311) | copy-start | bytes 100
  313.6 13.5 %copy-start.128 = (f32[8]{0:T(128)S(1)}, f32[8]{0:T(128)}, u32[]{:S(2)}) copy-start(f32[8]{0:T(128)} %constant.313) | copy-start | bytes 100
  324.7 8.8 %collective-permute-start.3 = (f32[5,8,128]{2,1,0:T(8,128)S(1)}, f32[5,8,128]{2,1,0:T(8,128)S(1)}, u32[]{:S(2)}, u32[]{:S(2)}) collective-permute-start(f32[5,8,128]{2,1,0:T(8,128)S(1)} %fusion.52), channel_id=1, source_target_pairs={{496,0},{0,16},{16,32},{32,48},{48,64},{64,80},{80,96},{96,112},{1... | collective-permute-start | bytes 61448 | tf_op jit(solution)/shard_map/ppermute | solution.py:24
  327.2 6.6 %copy-start.2 = (f32[5,8,128,4]{1,3,2,0:T(4,128)S(1)}, f32[5,8,128,4]{1,3,2,0:T(4,128)}, u32[]{:S(2)}) copy-start(f32[5,8,128,4]{1,3,2,0:T(4,128)} %copy.969) | copy-start | bytes 245764
  (86 other events, 286.3 us)
where the time goes:
time: 348 us; the launch traced here: 344 us
  blocking collectives  106 us (30%)
  other arithmetic  104 us (30%)
  local copies, waits for them, and re-layouts  91 us (26%)
  starting transfers between devices  16.1 us (5%)
  between operations  13.4 us (4%)
  matrix products  12.8 us (4%)
    psum x1, blocking collectives, on_device(): totals = lax.psum(wall_loads, ('azim', 'axial', 'radial'))  106 us
    unnamed x32, other arithmetic  33.5 us
    dot_general x12, matrix products, element_mix(): jnp.einsum(patterns[direction], jnp.asarray(matrix, jnp.float32), values....  11 us
    concatenate x18, local copies, waits for them, and re-layouts, element_mix(): jnp.roll(values, -offset, axis=direction)  10.1 us
    add x6, other arithmetic, element_mix(): total_sum + jnp.asarray(factor, jnp.float32) * jnp.roll(values, -offset,...  9.62 us
    mul x6, local copies, waits for them, and re-layouts, element_mix(): jnp.asarray(factor, jnp.float32) * jnp.roll(values, -offset, axis=direction)  9.56 us
    unnamed x306, local copies, waits for them, and re-layouts  9.48 us
    another operation x10, other arithmetic, normal_flux(): jnp.stack([conserved[0] * relative, conserved[1] * relative + pressure *...  9.38 us
  transfers between devices with their start and end apart: 6, of which 0 were waited for; matrix products, arithmetic and copies ran while one was open for 45% of the time, Pallas kernels for 0%

commit v1 on v0

v1 whole, which is shorter than its diff:
```python
import math

import jax
import jax.numpy as jnp
import numpy as np
from jax import lax
from jax.experimental import pallas as pl
from jax.experimental.pallas import tpu as pltpu
from jax.sharding import PartitionSpec as P

MESH = pl.DeviceIdType.MESH
F32 = jnp.float32

AZIM, AXIAL, RADIAL = 32, 8, 2
ROOT = 1
STEP_A = 2.0 * math.pi / 32
STEP_Z = 8.0 / 16
STEP_R = 2.0 / 64
DT = 0.05 * min(STEP_R, STEP_Z, STEP_A)
FREE = (1.0, 0.0, 0.0, 0.5, 1.0 / (1.4 * 0.4) + 0.125)


def fr_tables():
    outer_point = np.sqrt(3.0 / 7.0 + 2.0 / 7.0 * np.sqrt(6.0 / 5.0))
    inner_point = np.sqrt(3.0 / 7.0 - 2.0 / 7.0 * np.sqrt(6.0 / 5.0))
    points = np.array([-outer_point, -inner_point, inner_point, outer_point])
    outer_weight = (18.0 - np.sqrt(30.0)) / 36.0
    inner_weight = (18.0 + np.sqrt(30.0)) / 36.0
    weights = np.array([outer_weight, inner_weight, inner_weight, outer_weight])
    bary_weights = np.array(
        [1.0 / np.prod([points[i] - points[j] for j in range(4) if j != i]) for i in range(4)]
    )
    derivative = np.zeros((4, 4))
    for i in range(4):
        for j in range(4):
            if i != j:
                derivative[i, j] = bary_weights[j] / bary_weights[i] / (points[i] - points[j])
        derivative[i, i] = -np.sum(derivative[i])

    def basis_at(location):
        return np.array(
            [
                np.prod(
                    [(location - points[j]) / (points[i] - points[j]) for j in range(4) if j != i]
                )
                for i in range(4)
            ]
        )

    at_lower = basis_at(-1.0)
    at_upper = basis_at(1.0)
    third_slope = 0.5 * (15.0 * points * points - 3.0)
    fourth_slope = 0.5 * (35.0 * points**3 - 15.0 * points)
    slope_left = 0.5 * (fourth_slope - third_slope)
    slope_right = 0.5 * (fourth_slope + third_slope)
    return (points, weights, derivative, at_lower, at_upper, slope_left, slope_right)


X, Q, D, LA, LB, SC, SE = fr_tables()
OFF = (X + 1.0) / 2.0
MIX = D - np.outer(SC, LA) - np.outer(SE, LB)


def radial_matrices():
    low, up, mean_own, mean_below, mix, corr = (np.zeros((128, 128)) for _ in range(6))
    for j in range(128):
        e, k = divmod(j, 4)
        below = 31 if j == 127 else e - 1
        for i in range(4):
            low[4 * e + i, j] = LA[i]
            mean_own[4 * e + i, j] = Q[i] / 2
            mix[4 * e + i, j] = MIX[k, i]
            if below >= 0:
                up[4 * below + i, j] = LB[i]
                mean_below[4 * below + i, j] = Q[i] / 2
        corr[4 * e, j] += SC[k]
        corr[127 if e == 31 else 4 * (e + 1), j] += SE[k]
    return np.concatenate([low, up, mean_own, mean_below, mix, corr], axis=1).astype(np.float32)


def axial_matrices():
    low, up, mean_low, mean_up, mix, corr = (np.zeros((8, 8)) for _ in range(6))
    for j in range(8):
        e, k = divmod(j, 4)
        own = None if j == 3 else e
        below = 1 if j == 3 else (0 if e == 1 else None)
        for i in range(4):
            if own is not None:
                low[j, 4 * own + i] = LA[i]
                mean_low[j, 4 * own + i] = Q[i] / 2
            if below is not None:
                up[j, 4 * below + i] = LB[i]
                mean_up[j, 4 * below + i] = Q[i] / 2
            mix[j, 4 * e + i] = MIX[k, i]
        corr[j, 4 * e] += SC[k]
        corr[j, 4 if e == 0 else 3] += SE[k]
    pack, pack_mean = np.zeros((8, 32)), np.zeros((8, 32))
    for a in range(4):
        for i in range(4):
            pack[a, 8 * a + i] = LA[i]
            pack[4 + a, 8 * a + 4 + i] = LB[i]
            pack_mean[a, 8 * a + i] = Q[i] / 2
            pack_mean[4 + a, 8 * a + 4 + i] = Q[i] / 2
    four = np.eye(4)
    parts = [np.kron(four, low), np.kron(four, up), pack]
    parts += [np.kron(four, mean_low), np.kron(four, mean_up), pack_mean]
    parts += [np.kron(four, mix), np.kron(four, corr)]
    return np.concatenate(parts, axis=0).astype(np.float32)


def angle_table():
    table = np.zeros((32, 128))
    for e in range(32):
        angles = np.array([*(e + OFF), e, e + 1.0]) * STEP_A
        table[e, 0:6] = np.cos(angles)
        table[e, 6:12] = np.sin(angles)
    return table.astype(np.float32)


def dot(a, b):
    return jnp.dot(a, b, precision=lax.Precision.HIGHEST, preferred_element_type=F32)


def weighed(factors, values):
    total = float(factors[0]) * values[0]
    for factor, value in zip(factors[1:], values[1:]):
        total = total + float(factor) * value
    return total


def pressure_of(u):
    return 0.4 * (u[4] - 0.5 * (u[1] * u[1] + u[2] * u[2] + u[3] * u[3]) / u[0])


def still_flux(u, normal):
    p = pressure_of(u)
    through = u[3] if normal is None else u[1] * normal[0] + u[2] * normal[1]
    vn = through / u[0]
    flux = [through, u[1] * vn, u[2] * vn, u[3] * vn, (u[4] + p) * vn]
    if normal is None:
        flux[3] = flux[3] + p
    else:
        flux[1] = flux[1] + p * normal[0]
        flux[2] = flux[2] + p * normal[1]
    return flux


def face_terms(minus, plus, bound, normal):
    low, high = still_flux(minus, normal), still_flux(plus, normal)
    half_jump = [0.5 * (b - a) for a, b in zip(minus, plus)]
    mean = [0.5 * (a + b) for a, b in zip(minus, plus)]
    base = [0.5 * (a + b) - bound * h for a, b, h in zip(low, high, half_jump)]
    return base, mean, half_jump


def section_kernel(
    rho_h, mom_h, ene_h, flag_h, body_h, radm_h, axm_h, ang_h,
    out_ref, body_ref,
    u_v, radm, axm, ang_s, flag_s, body_s,
    own, col, p1, p2, p3,
    azs_lo, azs_hi, azr_lo, azr_hi, axs, axr_lo, axr_hi, rads, radr,
    r0, br, cr, bz, cz, aface,
    load_sem, send_sem, recv_sem, ready_sem,
):
    az, ax, ra = lax.axis_index("azim"), lax.axis_index("axial"), lax.axis_index("radial")
    is_root = (ra == 0) & (ax == ROOT)
    is_near = (ra == 0) & (ax < 4) & (ax != ROOT)
    is_far = (ra == 0) & (ax >= 4)
    column_root = {"axial": ROOT, "radial": 0}

    loads = [
        pltpu.make_async_copy(src, dst, load_sem.at[i])
        for i, (src, dst) in enumerate(
            [
                (ang_h.at[pl.ds(az, 1)], ang_s),
                (flag_h, flag_s),
                (rho_h, u_v.at[0]),
                (mom_h, u_v.at[pl.ds(1, 3)]),
                (ene_h, u_v.at[4]),
                (radm_h, radm),
                (axm_h, axm),
                (body_h, body_s),
            ]
        )
    ]
    for load in loads:
        load.start()

    barrier = pltpu.get_barrier_semaphore()

    def greet(device):
        pl.semaphore_signal(barrier, inc=1, device_id=device, device_id_type=MESH)

    @pl.when(is_root)
    def _():
        def greet_column(i, carry):
            for k in (7, 6, 5, 4):
                greet({"azim": i, "axial": k, "radial": 0})
            return carry

        lax.fori_loop(0, AZIM, greet_column, 0)

        def greet_root(i, carry):
            greet({"azim": lax.rem(az + i, AZIM)})
            return carry

        lax.fori_loop(1, AZIM, greet_root, 0)
        for k in (0, 2, 3):
            greet({"axial": k})
        for k in range(AXIAL):
            greet({"axial": k, "radial": 1})

    below = lax.rem(az + (AZIM - 1), AZIM)
    above = lax.rem(az + 1, AZIM)
    greet({"azim": below})
    greet({"azim": above})

    @pl.when(ax > 0)
    def _():
        greet({"axial": ax - 1})

    @pl.when(ax < AXIAL - 1)
    def _():
        greet({"axial": ax + 1})

    @pl.when(ra == 0)
    def _():
        greet({"radial": 1})

    sub = lax.broadcasted_iota(jnp.int32, (8, 128), 0)
    lane = lax.broadcasted_iota(jnp.int32, (8, 128), 1)
    lane32 = lax.broadcasted_iota(jnp.int32, (32, 128), 1)
    sub32 = lax.broadcasted_iota(jnp.int32, (32, 128), 0) & 7

    def by_place(place, values):
        out = jnp.full(place.shape, float(values[3]), F32)
        for k in range(3):
            out = jnp.where(place == k, float(values[k]), out)
        return out

    z = ((ax * 2 + (sub >> 2)).astype(F32) + by_place(sub & 3, OFF)) * STEP_Z
    elem_r = (ra * 32 + (lane >> 2)).astype(F32)
    r = 1.0 + (elem_r + by_place(lane & 3, OFF)) * STEP_R
    r_face = 1.0 + (elem_r + jnp.where(lane == 127, 1.0, 0.0)) * STEP_R

    loads[0].wait()
    loads[1].wait()
    cos = [ang_s[0, k] for k in range(6)]
    sin = [ang_s[0, 6 + k] for k in range(6)]
    flag = jnp.where(
        sub < 4,
        jnp.full((8, 128), flag_s[0, 0], jnp.int32),
        jnp.full((8, 128), flag_s[0, 1], jnp.int32),
    ).astype(F32)
    area_z = flag * by_place(sub & 3, Q * (0.5 * STEP_Z))
    zero = jnp.zeros((8, 128), F32)
    load_w = []
    for a in range(4):
        arm = jnp.where(lane >= 2, z, 1.0) * area_z * float(Q[a] * (0.5 * STEP_A))
        turn = jnp.where((lane == 0) | (lane == 3), -cos[a], jnp.where(lane == 1, -sin[a], sin[a]))
        load_w.append(jnp.where(lane < 4, arm * turn, zero))
    load_w = jnp.concatenate(load_w, axis=0)
    wall_a = jnp.where(lane32 < 4, by_place(lane32 & 3, LA), 0.0)
    loads[2].wait()
    loads[3].wait()
    loads[4].wait()
    u = [u_v[f].reshape(32, 128) for f in range(5)]

    wall = [jnp.sum(x * wall_a, axis=1, keepdims=True) for x in u]
    own[...] = jnp.sum(pressure_of(wall) * load_w, axis=0, keepdims=True)

    greeted = 2 + jnp.where(ax > 0, 1, 0) + jnp.where(ax < AXIAL - 1, 1, 0)
    greeted = greeted + jnp.where(
        ra == 1, 2, jnp.where(ax == ROOT, AZIM - 1, jnp.where(ax >= 4, AZIM, 1))
    )
    pl.semaphore_wait(barrier, greeted)

    def push(src, dst, lane_of, device):
        return pltpu.make_async_remote_copy(
            src_ref=src,
            dst_ref=dst,
            send_sem=send_sem.at[lane_of],
            recv_sem=recv_sem.at[lane_of],
            device_id=device,
            device_id_type=MESH,
        )

    def arrived(ref, lane_of):
        pltpu.make_async_copy(ref, ref, recv_sem.at[lane_of]).wait()

    def left(ref, lane_of):
        pltpu.make_async_copy(ref, ref, send_sem.at[lane_of]).wait()

    @pl.when(is_far)
    def _():
        slot = az * 4 + (ax - 4)

        def send(i, carry):
            push(own, p2.at[slot], 1, {"azim": i, "axial": ROOT, "radial": 0}).start()
            return carry

        lax.fori_loop(0, AZIM, send, 0)

    @pl.when(is_near)
    def _():
        push(own, p1.at[jnp.where(ax == 0, 0, ax - 1)], 0, column_root).start()

    @pl.when(jnp.logical_not(is_root))
    def _():
        pl.semaphore_signal(ready_sem, inc=1, device_id=column_root, device_id_type=MESH)

    rho = u[0]
    p = pressure_of(u)
    sound = jnp.sqrt(1.4 * p / rho)
    cos32 = jnp.concatenate([jnp.full((8, 128), cos[a], F32) for a in range(4)], axis=0)
    sin32 = jnp.concatenate([jnp.full((8, 128), sin[a], F32) for a in range(4)], axis=0)
    speed_r = jnp.abs((u[1] * cos32 + u[2] * sin32) / rho) + sound
    speed_a = jnp.abs((u[2] * cos32 - u[1] * sin32) / rho) + sound
    speed_z = jnp.abs(u[3] / rho) + sound

    def rows(x):
        return [x[8 * a : 8 * a + 8] for a in range(4)]

    u_rows = [rows(x) for x in u]
    mean_a = weighed(Q / 2, rows(speed_a))
    for f in range(5):
        azs_lo[f] = weighed(LA, u_rows[f])
        azs_hi[f] = weighed(LB, u_rows[f])
    azs_lo[5] = mean_a
    azs_hi[5] = mean_a
    push(azs_lo, azr_hi, 3, {"azim": below}).start()
    push(azs_hi, azr_lo, 4, {"azim": above}).start()

    loads[5].wait()
    loads[6].wait()
    u_wide = jnp.concatenate(u, axis=1)
    ax_tr = dot(axm[0:72], u_wide)
    ax_sp = dot(axm[72:144], speed_z)
    for f in range(5):
        axs[f] = ax_tr[64:72, 128 * f : 128 * (f + 1)]
    axs[5] = ax_sp[64:72]

    @pl.when(ax > 0)
    def _():
        push(axs, axr_hi, 5, {"axial": ax - 1}).start()

    @pl.when(ax < AXIAL - 1)
    def _():
        push(axs, axr_lo, 6, {"axial": ax + 1}).start()

    rad_tr = dot(jnp.concatenate(u, axis=0), radm[:, 0:256])
    rad_sp = dot(speed_r, radm[:, 256:512])
    rad_lo = [rad_tr[32 * f : 32 * f + 32, 0:128] for f in range(5)] + [rad_sp[:, 0:128]]
    rad_up = [rad_tr[32 * f : 32 * f + 32, 128:256] for f in range(5)] + [rad_sp[:, 128:256]]
    inner = jnp.full((32, 128), ra, jnp.int32) == 0
    packed = jnp.zeros((32, 128), F32)
    for f in range(6):
        edge = jnp.where(
            inner,
            jnp.broadcast_to(rad_up[f][:, 127:128], (32, 128)),
            jnp.broadcast_to(rad_lo[f][:, 0:1], (32, 128)),
        )
        packed = jnp.where(lane32 == f, edge, packed)
    rads[...] = packed

    @pl.when(ra == 1)
    def _():
        push(rads, radr, 7, {"radial": 0}).start()

    r32 = jnp.concatenate([r] * 4, axis=0)
    rf32 = jnp.concatenate([r_face] * 4, axis=0)
    k_r = (DT * 2.0 / STEP_R) / r32
    k_a = (DT * 2.0 / STEP_A) / r
    k_a32 = jnp.concatenate([k_a] * 4, axis=0)
    k_z = DT * 2.0 / STEP_Z
    flux_r = still_flux(u, (cos32, sin32))
    flux_a = still_flux(u, (-sin32, cos32))
    flux_z = still_flux(u, None)
    mix_r = dot(
        jnp.concatenate([r32 * x for x in flux_r] + [r32 * x for x in u], axis=0), radm[:, 512:640]
    )
    mix_z = dot(axm[144:176], jnp.concatenate(flux_z + u, axis=1))
    for f in range(5):
        flux_rows = rows(flux_a[f])
        mix_a = jnp.concatenate([weighed(MIX[a], flux_rows) for a in range(4)], axis=0)
        r0[f] = (
            -k_r * mix_r[32 * f : 32 * f + 32]
            - k_a32 * mix_a
            - k_z * mix_z[:, 128 * f : 128 * f + 128]
        )
        br[f] = k_r * mix_r[160 + 32 * f : 192 + 32 * f]
        bz[f] = k_z * mix_z[:, 640 + 128 * f : 768 + 128 * f]

    @pl.when(is_root)
    def _():
        arrived(p1, 0)
        col[...] = own[...] + jnp.sum(p1[...], axis=0)

        def send(i, carry):
            push(col, p2.at[4 * AZIM - 1 + i], 1, {"azim": lax.rem(az + i, AZIM)}).start()
            return carry

        lax.fori_loop(1, AZIM, send, 0)

    arrived(azr_lo, 4)
    arrived(azr_hi, 3)
    own_lo = [azs_lo[f] for f in range(6)]
    own_hi = [azs_hi[f] for f in range(6)]
    from_lo = [azr_lo[f] for f in range(6)]
    from_hi = [azr_hi[f] for f in range(6)]
    lo_terms = face_terms(
        from_lo[:5], own_lo[:5], jnp.maximum(from_lo[5], own_lo[5]), (-sin[4], cos[4])
    )
    hi_terms = face_terms(
        own_hi[:5], from_hi[:5], jnp.maximum(from_hi[5], own_hi[5]), (-sin[5], cos[5])
    )
    for f in range(5):
        for a in range(4):
            fix = float(SC[a]) * lo_terms[0][f] + float(SE[a]) * hi_terms[0][f]
            r0[f, 8 * a : 8 * a + 8] = r0[f, 8 * a : 8 * a + 8] - k_a * fix
        aface[f] = k_a * lo_terms[1][f]
        aface[5 + f] = k_a * lo_terms[2][f]
        aface[10 + f] = k_a * hi_terms[1][f]
        aface[15 + f] = k_a * hi_terms[2][f]

    @pl.when(ax > 0)
    def _():
        arrived(axr_lo, 6)

    @pl.when(ax == 0)
    def _():
        for f in range(6):
            axr_lo[f] = jnp.full((8, 128), (*FREE, 1.5)[f], F32)

    @pl.when(ax < AXIAL - 1)
    def _():
        arrived(axr_hi, 5)

    @pl.when(ax == AXIAL - 1)
    def _():
        for f in range(6):
            axr_hi[f] = jnp.full((8, 128), (*FREE, 1.5)[f], F32)

    def spread(ref, f, first):
        got = ref[f]
        return jnp.concatenate(
            [jnp.broadcast_to(got[first + a : first + a + 1], (8, 128)) for a in range(4)], axis=0
        )

    minus, plus = [], []
    for f in range(6):
        if f < 5:
            low, up = (ax_tr[32 * i : 32 * i + 32, 128 * f : 128 * f + 128] for i in range(2))
        else:
            low, up = ax_sp[0:32], ax_sp[32:64]
        minus.append(jnp.where(sub32 < 3, spread(axr_lo, f, 4), up))
        plus.append(jnp.where(sub32 == 3, spread(axr_hi, f, 0), low))
    terms = face_terms(minus[:5], plus[:5], jnp.maximum(minus[5], plus[5]), None)
    fix_z = dot(axm[176:208], jnp.concatenate(terms[0] + terms[1] + terms[2], axis=1))
    for f in range(5):
        r0[f] = r0[f] - k_z * fix_z[:, 128 * f : 128 * f + 128]
        bz[f] = bz[f] + k_z * fix_z[:, 640 + 128 * f : 768 + 128 * f]
        cz[f] = k_z * fix_z[:, 1280 + 128 * f : 1408 + 128 * f]

    arrived(radr, 7)

    @pl.when(ra == 0)
    def _():
        push(rads, radr, 7, {"radial": 1}).start()

    lowest = lane32 < 4
    highest = lane32 == 127
    minus, plus = [], []
    got = radr[...]
    for f in range(6):
        ghost = jnp.broadcast_to(got[:, f : f + 1], (32, 128))
        minus.append(jnp.where(lowest, jnp.where(inner, rad_lo[f], ghost), rad_up[f]))
        free = (*FREE, 1.0)[f]
        plus.append(jnp.where(highest, jnp.where(inner, ghost, free), rad_lo[f]))
    base, mean, half_jump = face_terms(
        minus[:5], plus[:5], jnp.maximum(minus[5], plus[5]), (cos32, sin32)
    )
    at_wall = lowest & inner
    pw = pressure_of(plus[:5])
    wall_base = [0.0, pw * cos32, pw * sin32, 0.0, 0.0]
    wall_mean = [0.0, 0.0, 0.0, 0.0, -pw]
    base = [rf32 * jnp.where(at_wall, w, x) for w, x in zip(wall_base, base)]
    mean = [rf32 * jnp.where(at_wall, w, x) for w, x in zip(wall_mean, mean)]
    half_jump = [rf32 * jnp.where(at_wall, 0.0, x) for x in half_jump]
    fix_r = dot(jnp.concatenate(base + mean + half_jump, axis=0), radm[:, 640:768])
    for f in range(5):
        r0[f] = r0[f] - k_r * fix_r[32 * f : 32 * f + 32]
        br[f] = br[f] + k_r * fix_r[160 + 32 * f : 192 + 32 * f]
        cr[f] = k_r * fix_r[320 + 32 * f : 352 + 32 * f]

    loads[7].wait()

    @pl.when(is_root)
    def _():
        pl.semaphore_wait(ready_sem, 2 * AXIAL - 1)
        arrived(p2, 1)
        p3[...] = col[...] + jnp.sum(p2[...], axis=0)
        for k in (2, 0, 3, 4, 5, 6, 7):
            push(p3, p3, 2, {"axial": k}).start()
        for k in range(AXIAL):
            push(p3, p3, 2, {"axial": k, "radial": 1}).start()

    @pl.when(jnp.logical_not(is_root))
    def _():
        arrived(p3, 2)

    total = p3[...]
    load = [jnp.broadcast_to(total[:, i : i + 1], (8, 128)) for i in range(4)]
    v = [body_s[0, i] for i in range(3)]
    om = [body_s[0, 3 + i] for i in range(3)]
    spin = [om[0], om[1], 0.25 * om[2]]
    gyro = [
        om[1] * spin[2] - om[2] * spin[1],
        om[2] * spin[0] - om[0] * spin[2],
        om[0] * spin[1] - om[1] * spin[0],
    ]
    v0 = v[0] + 60.0 * load[0]
    v1 = v[1] + 60.0 * load[1]
    v2 = jnp.full((8, 128), v[2], F32)
    o0 = om[0] + 30.0 * (load[2] - gyro[0])
    o1 = om[1] + 30.0 * (load[3] - gyro[1])
    o2 = jnp.full((8, 128), om[2] - 120.0 * gyro[2], F32)
    body_row = zero
    for i, value in enumerate((v0, v1, v2, o0, o1, o2)):
        body_row = jnp.where(lane == i, value, body_row)
    body_ref[...] = body_row[0:1, 0:6]

    along_x = v0 + z * o1
    along_y = v1 - z * o0
    swirl = o2 * r

    def azim_speed(k):
        return cos[k] * along_y - sin[k] * along_x + swirl

    s_a = [azim_speed(k) for k in range(4)]
    s_lo, s_hi = azim_speed(4), azim_speed(5)
    s_r = [cos[a] * along_x + sin[a] * along_y for a in range(4)]
    s_z = [v2 + r * (o0 * sin[a] - o1 * cos[a]) for a in range(4)]
    d0, d1, d2 = DT * o0, DT * o1, DT * o2
    for f in range(5):
        carried = [k_a * s_a[k] * u_v[f, k] for k in range(4)]
        at_lo = s_lo * aface[f] + jnp.abs(s_lo) * aface[5 + f]
        at_hi = s_hi * aface[10 + f] + jnp.abs(s_hi) * aface[15 + f]
        for a in range(4):
            row = slice(8 * a, 8 * a + 8)
            value = r0[f, row] + s_r[a] * br[f, row] + jnp.abs(s_r[a]) * cr[f, row]
            value = value + s_z[a] * bz[f, row] + jnp.abs(s_z[a]) * cz[f, row]
            value = value + weighed(MIX[a], carried)
            value = value + float(SC[a]) * at_lo + float(SE[a]) * at_hi
            if f == 1:
                value = value - (d1 * u_v[3, a] - d2 * u_v[2, a])
            if f == 2:
                value = value - (d2 * u_v[1, a] - d0 * u_v[3, a])
            if f == 3:
                value = value - (d0 * u_v[2, a] - d1 * u_v[1, a])
            out_ref[f, a] = value

    @pl.when(is_root)
    def _():
        left(p2.at[pl.ds(0, AZIM - 1)], 1)
        left(p2.at[pl.ds(0, 2 * AXIAL - 1)], 2)

    @pl.when(is_far)
    def _():
        left(p2.at[pl.ds(0, AZIM)], 1)

    @pl.when(is_near)
    def _():
        left(own, 0)

    left(azs_lo, 3)
    left(azs_hi, 4)

    @pl.when(ax > 0)
    def _():
        left(axs, 5)

    @pl.when(ax < AXIAL - 1)
    def _():
        left(axs, 6)

    left(rads, 7)


def store_kernel(out_ref, body_ref, rho_h, mom_h, ene_h, body_h, sems):
    copies = [
        pltpu.make_async_copy(src, dst, sems.at[i])
        for i, (src, dst) in enumerate(
            [
                (out_ref.at[pl.ds(1, 3)], mom_h),
                (out_ref.at[0], rho_h),
                (out_ref.at[4], ene_h),
                (body_ref, body_h),
            ]
        )
    ]
    for copy in copies:
        copy.start()
    for copy in copies:
        copy.wait()


def on_device(density, momentum, energy, wall_flags, body_motion):
    block = density.shape
    hbm = pl.BlockSpec(memory_space=pl.ANY)
    vmem = pl.BlockSpec(memory_space=pltpu.VMEM)
    halo = pltpu.VMEM((6, 8, 128), F32)
    part = pltpu.VMEM((5, 32, 128), F32)
    increment, body_row = pl.pallas_call(
        section_kernel,
        out_shape=(pltpu.VMEM((5, *block), F32), pltpu.VMEM((1, 6), F32)),
        in_specs=[hbm] * 8,
        out_specs=(vmem, vmem),
        scratch_shapes=[
            pltpu.VMEM((5, *block), F32),
            pltpu.VMEM((128, 768), F32),
            pltpu.VMEM((208, 32), F32),
            pltpu.SMEM((1, 128), F32),
            pltpu.SMEM((1, 2), jnp.int32),
            pltpu.SMEM((1, 6), F32),
            pltpu.VMEM((1, 128), F32),
            pltpu.VMEM((1, 128), F32),
            pltpu.VMEM((3, 1, 128), F32),
            pltpu.VMEM((5 * AZIM - 1, 1, 128), F32),
            pltpu.VMEM((1, 128), F32),
            *[halo] * 7,
            pltpu.VMEM((32, 128), F32),
            pltpu.VMEM((32, 128), F32),
            *[part] * 5,
            pltpu.VMEM((20, 8, 128), F32),
            pltpu.SemaphoreType.DMA((8,)),
            pltpu.SemaphoreType.DMA((8,)),
            pltpu.SemaphoreType.DMA((8,)),
            pltpu.SemaphoreType.REGULAR,
        ],
        compiler_params=pltpu.CompilerParams(
            collective_id=0, has_side_effects=True
        ),
    )(
        density,
        momentum,
        energy,
        wall_flags,
        body_motion.reshape(1, 6),
        jnp.asarray(radial_matrices()),
        jnp.asarray(axial_matrices()),
        jnp.asarray(angle_table()),
    )
    increment = pltpu.with_memory_space_constraint(increment, pltpu.VMEM)
    body_row = pltpu.with_memory_space_constraint(body_row, pltpu.VMEM)
    rho, mom, ene, body = pl.pallas_call(
        store_kernel,
        out_shape=(
            jax.ShapeDtypeStruct(block, F32),
            jax.ShapeDtypeStruct((3, *block), F32),
            jax.ShapeDtypeStruct(block, F32),
            jax.ShapeDtypeStruct((1, 6), F32),
        ),
        in_specs=[vmem, vmem],
        out_specs=[hbm] * 4,
        scratch_shapes=[pltpu.SemaphoreType.DMA((4,))],
    )(increment, body_row)
    return rho, mom, ene, body.reshape(6)


def solution(mesh):
    return jax.shard_map(
        on_device,
        mesh=mesh,
        in_specs=(
            P("azim", "axial", "radial"),
            P(None, "azim", "axial", "radial"),
            P("azim", "axial", "radial"),
            P("azim", "axial"),
            P(),
        ),
        out_specs=(
            P("azim", "axial", "radial"),
            P(None, "azim", "axial", "radial"),
            P("azim", "axial", "radial"),
            P(),
        ),
        check_vma=False,
    )
```

time: 348 us -> 20.9 us (0.06); the launches traced: 344 us -> 20.7 us
  blocking collectives: 106 us -> 0 us
  other arithmetic: 104 us -> 0 us
  local copies, waits for them, and re-layouts: 91 us -> 0 us
  Pallas kernels: 0 us -> 20.1 us
  starting transfers between devices: 16.1 us -> 0 us
  matrix products: 12.8 us -> 0 us
  between operations: 13.4 us -> 0.64 us
    psum x1 -> x0, blocking collectives: 106 us -> none  [on_device(): totals = lax.psum(wall_loads, ('azim', 'axial', 'radial'))]
    unnamed x32 -> x0, other arithmetic: 33.5 us -> none
    add x16 -> x0, other arithmetic: 28.2 us -> none  [the longest x6 9.62 us: element_mix(): total_sum + jnp.asarray(factor, jnp.float32) * jnp.roll(values, -offset,...]
    pallas_call x0 -> x2, Pallas kernels: none -> 20.1 us  [the longest x1 19.4 us: on_device(): pl.pallas_call(section_kernel, out_shape=(pltpu.VMEM((5, *block), F32), p...]
    mul x17 -> x0, other arithmetic: 17.2 us -> none  [the longest x7 7.1 us: rusanov(): return metric * (average - 0.5 * wave_bound * (plus_side - minus_side))]
    slice x24 -> x0, local copies, waits for them, and re-layouts: 17.2 us -> none  [the longest x12 8.71 us: element_mix(): jnp.roll(values, -offset, axis=direction)]
    ppermute x6 -> x0, starting transfers between devices: 16.1 us -> none  [the longest x2 7.03 us: with_halo(): lax.ppermute(tail, axis, [(i, (i + 1) % count) for i in range(ends)])]
    add x18 -> x0, local copies, waits for them, and re-layouts: 13.6 us -> none  [the longest x6 8.06 us: element_mix(): total_sum + jnp.asarray(factor, jnp.float32) * jnp.roll(values, -offset,...]
  transfers between devices with their start and end apart: 6 -> 0, of which waited for: 0 -> 0; matrix products, arithmetic and copies ran while one was open for 45% -> 0% of each run, Pallas kernels for 0% -> 0%
where the time goes in v1:
time: 20.9 us; the launch traced here: 20.7 us
  Pallas kernels  20.1 us (96%)
  between operations  0.64 us (3%)
    pallas_call x1, Pallas kernels, on_device(): pl.pallas_call(section_kernel, out_shape=(pltpu.VMEM((5, *block), F32), p...  19.4 us
    pallas_call x1, Pallas kernels, on_device(): pl.pallas_call(store_kernel, out_shape=(jax.ShapeDtypeStruct(block, F32),...  0.67 us

profile of v1, /device:TPU:1, one launch (start us, length us, event | category | flops | bytes accessed | tf_op | source)
XLA Modules:
  0.0 20.7 jit_solution(9852615901616940390)
XLA Ops:
  0.6 19.4 %shard_map.111 = (f32[5,4,8,128]{3,2,1,0:T(8,128)S(1)}, f32[1,6]{1,0:T(1,128)S(1)}) custom-call(f32[4,8,128]{2,1,0:T(8,128)} %rho_h.1, f32[3,4,8,128]{3,2,1,0:T(8,128)} %mom_h.1, f32[4,8,128]{2,1,0:T(8,128)} %ene_h.1, s32[1,2]{1,0:T(1,128)} %flag_h.1, f32[1,6]{1,0:T(1,128)} %bitcast.2, f32[128,768]{1,0:T(8,128)} %constant.6.clone.radm_h, ...), custom_call_target="tpu_custom_call" | custom-call | tf_op jit(solution)/shard_map/pallas_call | solution.py:614
  20.0 0.7 %shard_map.112 = (f32[4,8,128]{2,1,0:T(8,128)}, f32[3,4,8,128]{3,2,1,0:T(8,128)}, f32[4,8,128]{2,1,0:T(8,128)}, f32[1,6]{1,0:T(1,128)}) custom-call(f32[5,4,8,128]{3,2,1,0:T(8,128)S(1)} %get-tuple-element.10.out_ref, f32[1,6]{1,0:T(1,128)S(1)} %get-tuple-element.11.body_ref), custom_call_target="tpu_custom_call" | custom-call | tf_op jit(solution)/shard_map/pallas_call | solution.py:656

commit v2 on v1

--- a/solution.py
+++ b/solution.py
@@ -164,8 +164,11 @@
 ):
     az, ax, ra = lax.axis_index("azim"), lax.axis_index("axial"), lax.axis_index("radial")
     is_root = (ra == 0) & (ax == ROOT)
+    is_relay = (ra == 0) & (ax == 0)
     is_near = (ra == 0) & (ax < 4) & (ax != ROOT)
     is_far = (ra == 0) & (ax >= 4)
+    is_even = lax.rem(az, 2) == 0
+    on_odd_core = lax.rem(ax, 2) == 1
     column_root = {"axial": ROOT, "radial": 0}
 
     loads = [
@@ -212,14 +215,16 @@
 
     below = lax.rem(az + (AZIM - 1), AZIM)
     above = lax.rem(az + 1, AZIM)
-    greet({"azim": below})
-    greet({"azim": above})
-
-    @pl.when(ax > 0)
+    @pl.when(is_even)
+    def _():
+        greet({"azim": below})
+        greet({"azim": above})
+
+    @pl.when(on_odd_core)
     def _():
         greet({"axial": ax - 1})
 
-    @pl.when(ax < AXIAL - 1)
+    @pl.when(on_odd_core & (ax < AXIAL - 1))
     def _():
         greet({"axial": ax + 1})
 
@@ -269,7 +274,8 @@
     wall = [jnp.sum(x * wall_a, axis=1, keepdims=True) for x in u]
     own[...] = jnp.sum(pressure_of(wall) * load_w, axis=0, keepdims=True)
 
-    greeted = 2 + jnp.where(ax > 0, 1, 0) + jnp.where(ax < AXIAL - 1, 1, 0)
+    greeted = jnp.where(is_even, 0, 2)
+    greeted = greeted + jnp.where(on_odd_core, 0, jnp.where(ax > 0, 2, 1))
     greeted = greeted + jnp.where(
         ra == 1, 2, jnp.where(ax == ROOT, AZIM - 1, jnp.where(ax >= 4, AZIM, 1))
     )
@@ -328,8 +334,12 @@
         azs_hi[f] = weighed(LB, u_rows[f])
     azs_lo[5] = mean_a
     azs_hi[5] = mean_a
-    push(azs_lo, azr_hi, 3, {"azim": below}).start()
-    push(azs_hi, azr_lo, 4, {"azim": above}).start()
+
+    def push_azim():
+        push(azs_lo, azr_hi, 3, {"azim": below}).start()
+        push(azs_hi, azr_lo, 4, {"azim": above}).start()
+
+    pl.when(jnp.logical_not(is_even))(push_azim)
 
     loads[5].wait()
     loads[6].wait()
@@ -340,13 +350,14 @@
         axs[f] = ax_tr[64:72, 128 * f : 128 * (f + 1)]
     axs[5] = ax_sp[64:72]
 
-    @pl.when(ax > 0)
-    def _():
+    def push_axial_down():
         push(axs, axr_hi, 5, {"axial": ax - 1}).start()
 
-    @pl.when(ax < AXIAL - 1)
-    def _():
+    def push_axial_up():
         push(axs, axr_lo, 6, {"axial": ax + 1}).start()
+
+    pl.when(jnp.logical_not(on_odd_core) & (ax > 0))(push_axial_down)
+    pl.when(jnp.logical_not(on_odd_core))(push_axial_up)
 
     rad_tr = dot(jnp.concatenate(u, axis=0), radm[:, 0:256])
     rad_sp = dot(speed_r, radm[:, 256:512])
@@ -366,6 +377,17 @@
     @pl.when(ra == 1)
     def _():
         push(rads, radr, 7, {"radial": 0}).start()
+
+    @pl.when(is_root)
+    def _():
+        arrived(p1, 0)
+        col[...] = own[...] + jnp.sum(p1[...], axis=0)
+
+        def send(i, carry):
+            push(col, p2.at[4 * AZIM - 1 + i], 1, {"azim": lax.rem(az + i, AZIM)}).start()
+            return carry
+
+        lax.fori_loop(1, AZIM, send, 0)
 
     r32 = jnp.concatenate([r] * 4, axis=0)
     rf32 = jnp.concatenate([r_face] * 4, axis=0)
@@ -391,19 +413,9 @@
         br[f] = k_r * mix_r[160 + 32 * f : 192 + 32 * f]
         bz[f] = k_z * mix_z[:, 640 + 128 * f : 768 + 128 * f]
 
-    @pl.when(is_root)
-    def _():
-        arrived(p1, 0)
-        col[...] = own[...] + jnp.sum(p1[...], axis=0)
-
-        def send(i, carry):
-            push(col, p2.at[4 * AZIM - 1 + i], 1, {"azim": lax.rem(az + i, AZIM)}).start()
-            return carry
-
-        lax.fori_loop(1, AZIM, send, 0)
-
     arrived(azr_lo, 4)
     arrived(azr_hi, 3)
+    pl.when(is_even)(push_azim)
     own_lo = [azs_lo[f] for f in range(6)]
     own_hi = [azs_hi[f] for f in range(6)]
     from_lo = [azr_lo[f] for f in range(6)]
@@ -426,6 +438,7 @@
     @pl.when(ax > 0)
     def _():
         arrived(axr_lo, 6)
+        pl.when(on_odd_core)(push_axial_down)
 
     @pl.when(ax == 0)
     def _():
@@ -435,6 +448,7 @@
     @pl.when(ax < AXIAL - 1)
     def _():
         arrived(axr_hi, 5)
+        pl.when(on_odd_core)(push_axial_up)
 
     @pl.when(ax == AXIAL - 1)
     def _():
@@ -499,15 +513,25 @@
     def _():
         pl.semaphore_wait(ready_sem, 2 * AXIAL - 1)
         arrived(p2, 1)
-        p3[...] = col[...] + jnp.sum(p2[...], axis=0)
-        for k in (2, 0, 3, 4, 5, 6, 7):
+        sums = [p2[i] for i in range(8)]
+        for i in range(8, 5 * AZIM - 1):
+            sums[i % 8] = sums[i % 8] + p2[i]
+        while len(sums) > 1:
+            sums = [x + y for x, y in zip(sums[0::2], sums[1::2])]
+        p3[...] = col[...] + sums[0]
+        for k in (2, 3, 0):
+            push(p3, p3, 2, {"axial": k}).start()
+
+    @pl.when(jnp.logical_not(is_root))
+    def _():
+        arrived(p3, 2)
+
+    @pl.when(is_relay)
+    def _():
+        for k in (4, 5, 6, 7):
             push(p3, p3, 2, {"axial": k}).start()
         for k in range(AXIAL):
             push(p3, p3, 2, {"axial": k, "radial": 1}).start()
-
-    @pl.when(jnp.logical_not(is_root))
-    def _():
-        arrived(p3, 2)
 
     total = p3[...]
     load = [jnp.broadcast_to(total[:, i : i + 1], (8, 128)) for i in range(4)]
@@ -563,7 +587,11 @@
     @pl.when(is_root)
     def _():
         left(p2.at[pl.ds(0, AZIM - 1)], 1)
-        left(p2.at[pl.ds(0, 2 * AXIAL - 1)], 2)
+        left(p2.at[pl.ds(0, 3)], 2)
+
+    @pl.when(is_relay)
+    def _():
+        left(p2.at[pl.ds(0, AXIAL + 4)], 2)
 
     @pl.when(is_far)
     def _():

time: 20.9 us -> 20.2 us (0.967)
  Pallas kernels: 20.1 us -> 19.4 us
    pallas_call x1, Pallas kernels: 19.4 us -> 18.8 us  [on_device(): pl.pallas_call(section_kernel, out_shape=(pltpu.VMEM((5, *block), F32), p...]
where the time goes in v2:
time: 20.2 us; the launch traced here: 20.1 us
  Pallas kernels  19.4 us (96%)
  between operations  0.64 us (3%)
    pallas_call x1, Pallas kernels, on_device(): pl.pallas_call(section_kernel, out_shape=(pltpu.VMEM((5, *block), F32), p...  18.8 us
    pallas_call x1, Pallas kernels, on_device(): pl.pallas_call(store_kernel, out_shape=(jax.ShapeDtypeStruct(block, F32),...  0.67 us

profile of v2, /device:TPU:1, one launch (start us, length us, event | category | flops | bytes accessed | tf_op | source)
XLA Modules:
  0.0 20.1 jit_solution(7031476803011027311)
XLA Ops:
  0.6 18.8 %shard_map.111 = (f32[5,4,8,128]{3,2,1,0:T(8,128)S(1)}, f32[1,6]{1,0:T(1,128)S(1)}) custom-call(f32[4,8,128]{2,1,0:T(8,128)} %rho_h.1, f32[3,4,8,128]{3,2,1,0:T(8,128)} %mom_h.1, f32[4,8,128]{2,1,0:T(8,128)} %ene_h.1, s32[1,2]{1,0:T(1,128)} %flag_h.1, f32[1,6]{1,0:T(1,128)} %bitcast.2, f32[128,768]{1,0:T(8,128)} %constant.6.clone.radm_h, ...), custom_call_target="tpu_custom_call" | custom-call | tf_op jit(solution)/shard_map/pallas_call | solution.py:642
  19.4 0.7 %shard_map.112 = (f32[4,8,128]{2,1,0:T(8,128)}, f32[3,4,8,128]{3,2,1,0:T(8,128)}, f32[4,8,128]{2,1,0:T(8,128)}, f32[1,6]{1,0:T(1,128)}) custom-call(f32[5,4,8,128]{3,2,1,0:T(8,128)S(1)} %get-tuple-element.10.out_ref, f32[1,6]{1,0:T(1,128)S(1)} %get-tuple-element.11.body_ref), custom_call_target="tpu_custom_call" | custom-call | tf_op jit(solution)/shard_map/pallas_call | solution.py:684

commit v3 on v2

--- a/solution.py
+++ b/solution.py
@@ -13,6 +13,7 @@
 
 AZIM, AXIAL, RADIAL = 32, 8, 2
 ROOT = 1
+EXTRA = 3
 STEP_A = 2.0 * math.pi / 32
 STEP_Z = 8.0 / 16
 STEP_R = 2.0 / 64
@@ -157,19 +158,23 @@
     rho_h, mom_h, ene_h, flag_h, body_h, radm_h, axm_h, ang_h,
     out_ref, body_ref,
     u_v, radm, axm, ang_s, flag_s, body_s,
-    own, col, p1, p2, p3,
+    own, col, p1, p2a, p2b, p3,
     azs_lo, azs_hi, azr_lo, azr_hi, axs, axr_lo, axr_hi, rads, radr,
     r0, br, cr, bz, cz, aface,
     load_sem, send_sem, recv_sem, ready_sem,
 ):
     az, ax, ra = lax.axis_index("azim"), lax.axis_index("axial"), lax.axis_index("radial")
     is_root = (ra == 0) & (ax == ROOT)
-    is_relay = (ra == 0) & (ax == 0)
     is_near = (ra == 0) & (ax < 4) & (ax != ROOT)
+    first_column = az == 0
+    is_extra = first_column & (ra == 0) & (ax == EXTRA)
+    is_teller = is_extra | (is_root & jnp.logical_not(first_column))
     is_far = (ra == 0) & (ax >= 4)
     is_even = lax.rem(az, 2) == 0
     on_odd_core = lax.rem(ax, 2) == 1
     column_root = {"axial": ROOT, "radial": 0}
+    column_teller = {"axial": jnp.where(first_column, EXTRA, ROOT), "radial": 0}
+    extra = {"azim": 0, "axial": EXTRA, "radial": 0}
 
     loads = [
         pltpu.make_async_copy(src, dst, load_sem.at[i])
@@ -194,7 +199,7 @@
     def greet(device):
         pl.semaphore_signal(barrier, inc=1, device_id=device, device_id_type=MESH)
 
-    @pl.when(is_root)
+    @pl.when(is_root | is_extra)
     def _():
         def greet_column(i, carry):
             for k in (7, 6, 5, 4):
@@ -203,6 +208,8 @@
 
         lax.fori_loop(0, AZIM, greet_column, 0)
 
+    @pl.when(is_root)
+    def _():
         def greet_root(i, carry):
             greet({"azim": lax.rem(az + i, AZIM)})
             return carry
@@ -210,6 +217,19 @@
         lax.fori_loop(1, AZIM, greet_root, 0)
         for k in (0, 2, 3):
             greet({"axial": k})
+
+    @pl.when(is_extra)
+    def _():
+        def greet_root(i, carry):
+            greet({"azim": i, "axial": ROOT})
+            return carry
+
+        lax.fori_loop(0, AZIM, greet_root, 0)
+        for k in (0, 2):
+            greet({"axial": k})
+
+    @pl.when(is_teller)
+    def _():
         for k in range(AXIAL):
             greet({"axial": k, "radial": 1})
 
@@ -274,10 +294,11 @@
     wall = [jnp.sum(x * wall_a, axis=1, keepdims=True) for x in u]
     own[...] = jnp.sum(pressure_of(wall) * load_w, axis=0, keepdims=True)
 
+    by_column = jnp.where(first_column & (ax != EXTRA), 2, 1)
     greeted = jnp.where(is_even, 0, 2)
     greeted = greeted + jnp.where(on_odd_core, 0, jnp.where(ax > 0, 2, 1))
     greeted = greeted + jnp.where(
-        ra == 1, 2, jnp.where(ax == ROOT, AZIM - 1, jnp.where(ax >= 4, AZIM, 1))
+        ra == 1, 2, jnp.where(ax == ROOT, AZIM, jnp.where(ax >= 4, AZIM + 1, by_column))
     )
     pl.semaphore_wait(barrier, greeted)
 
@@ -297,23 +318,40 @@
     def left(ref, lane_of):
         pltpu.make_async_copy(ref, ref, send_sem.at[lane_of]).wait()
 
-    @pl.when(is_far)
-    def _():
-        slot = az * 4 + (ax - 4)
-
+    def tell_all(src, dst, lane_of, first):
         def send(i, carry):
-            push(own, p2.at[slot], 1, {"azim": i, "axial": ROOT, "radial": 0}).start()
+            push(src, dst, lane_of, {"azim": lax.rem(az + i, AZIM), "axial": ROOT, "radial": 0}).start()
             return carry
 
-        lax.fori_loop(0, AZIM, send, 0)
+        def send_direct(i, carry):
+            push(src, dst, lane_of, {"azim": i, "axial": ROOT, "radial": 0}).start()
+            return carry
+
+        if first:
+            push(src, dst, lane_of, extra).start()
+            lax.fori_loop(1, AZIM, send, 0)
+        else:
+            send_direct(0, 0)
+            push(src, dst, lane_of, extra).start()
+            lax.fori_loop(1, AZIM, send_direct, 0)
+
+    @pl.when(is_far & (ax >= 6))
+    def _():
+        tell_all(own, p2a.at[az * 2 + (ax - 6)], 1, False)
+
+    @pl.when(is_far & (ax < 6))
+    def _():
+        tell_all(own, p2b.at[az * 2 + (ax - 4)], 8, False)
 
     @pl.when(is_near)
     def _():
         push(own, p1.at[jnp.where(ax == 0, 0, ax - 1)], 0, column_root).start()
 
-    @pl.when(jnp.logical_not(is_root))
-    def _():
-        pl.semaphore_signal(ready_sem, inc=1, device_id=column_root, device_id_type=MESH)
+    is_told = jnp.logical_not(is_root | is_extra)
+
+    @pl.when(is_told)
+    def _():
+        pl.semaphore_signal(ready_sem, inc=1, device_id=column_teller, device_id_type=MESH)
 
     rho = u[0]
     p = pressure_of(u)
@@ -382,12 +420,8 @@
     def _():
         arrived(p1, 0)
         col[...] = own[...] + jnp.sum(p1[...], axis=0)
-
-        def send(i, carry):
-            push(col, p2.at[4 * AZIM - 1 + i], 1, {"azim": lax.rem(az + i, AZIM)}).start()
-            return carry
-
-        lax.fori_loop(1, AZIM, send, 0)
+        p2b[2 * AZIM + az] = col[...]
+        tell_all(col, p2b.at[2 * AZIM + az], 8, True)
 
     r32 = jnp.concatenate([r] * 4, axis=0)
     rf32 = jnp.concatenate([r_face] * 4, axis=0)
@@ -511,27 +545,48 @@
 
     @pl.when(is_root)
     def _():
+        arrived(p2b.at[pl.ds(0, 3 * AZIM - 1)], 8)
+
+    @pl.when(is_extra)
+    def _():
+        arrived(p2b, 8)
+
+    @pl.when(is_extra)
+    def _():
+        pl.semaphore_wait(ready_sem, 2 * AXIAL - 2)
+
+    @pl.when(is_teller & is_root)
+    def _():
         pl.semaphore_wait(ready_sem, 2 * AXIAL - 1)
-        arrived(p2, 1)
-        sums = [p2[i] for i in range(8)]
-        for i in range(8, 5 * AZIM - 1):
-            sums[i % 8] = sums[i % 8] + p2[i]
+
+    def sum_rows(ref, count):
+        sums = [ref[i] for i in range(8)]
+        for i in range(8, count):
+            sums[i % 8] = sums[i % 8] + ref[i]
         while len(sums) > 1:
             sums = [x + y for x, y in zip(sums[0::2], sums[1::2])]
-        p3[...] = col[...] + sums[0]
-        for k in (2, 3, 0):
-            push(p3, p3, 2, {"axial": k}).start()
-
-    @pl.when(jnp.logical_not(is_root))
-    def _():
-        arrived(p3, 2)
-
-    @pl.when(is_relay)
-    def _():
-        for k in (4, 5, 6, 7):
+        return sums[0]
+
+    @pl.when(is_root | is_extra)
+    def _():
+        early = sum_rows(p2b, 3 * AZIM)
+        arrived(p2a, 1)
+        p3[...] = early + sum_rows(p2a, 2 * AZIM)
+
+    @pl.when(is_teller)
+    def _():
+        @pl.when(is_root)
+        def _():
+            push(p3, p3, 2, {"axial": EXTRA}).start()
+
+        for k in (2, 0, 4, 5, 6, 7):
             push(p3, p3, 2, {"axial": k}).start()
         for k in range(AXIAL):
             push(p3, p3, 2, {"axial": k, "radial": 1}).start()
+
+    @pl.when(is_told)
+    def _():
+        arrived(p3, 2)
 
     total = p3[...]
     load = [jnp.broadcast_to(total[:, i : i + 1], (8, 128)) for i in range(4)]
@@ -586,16 +641,23 @@
 
     @pl.when(is_root)
     def _():
-        left(p2.at[pl.ds(0, AZIM - 1)], 1)
-        left(p2.at[pl.ds(0, 3)], 2)
-
-    @pl.when(is_relay)
-    def _():
-        left(p2.at[pl.ds(0, AXIAL + 4)], 2)
-
-    @pl.when(is_far)
-    def _():
-        left(p2.at[pl.ds(0, AZIM)], 1)
+        left(p2b.at[pl.ds(0, AZIM)], 8)
+
+    @pl.when(is_teller & is_root)
+    def _():
+        left(p2b.at[pl.ds(0, 2 * AXIAL - 1)], 2)
+
+    @pl.when(is_extra)
+    def _():
+        left(p2b.at[pl.ds(0, 2 * AXIAL - 2)], 2)
+
+    @pl.when(is_far & (ax >= 6))
+    def _():
+        left(p2b.at[pl.ds(0, AZIM + 1)], 1)
+
+    @pl.when(is_far & (ax < 6))
+    def _():
+        left(p2b.at[pl.ds(0, AZIM + 1)], 8)
 
     @pl.when(is_near)
     def _():
@@ -654,7 +716,8 @@
             pltpu.VMEM((1, 128), F32),
             pltpu.VMEM((1, 128), F32),
             pltpu.VMEM((3, 1, 128), F32),
-            pltpu.VMEM((5 * AZIM - 1, 1, 128), F32),
+            pltpu.VMEM((2 * AZIM, 1, 128), F32),
+            pltpu.VMEM((3 * AZIM, 1, 128), F32),
             pltpu.VMEM((1, 128), F32),
             *[halo] * 7,
             pltpu.VMEM((32, 128), F32),
@@ -662,8 +725,8 @@
             *[part] * 5,
             pltpu.VMEM((20, 8, 128), F32),
             pltpu.SemaphoreType.DMA((8,)),
-            pltpu.SemaphoreType.DMA((8,)),
-            pltpu.SemaphoreType.DMA((8,)),
+            pltpu.SemaphoreType.DMA((9,)),
+            pltpu.SemaphoreType.DMA((9,)),
             pltpu.SemaphoreType.REGULAR,
         ],
         compiler_params=pltpu.CompilerParams(

time: 20.2 us -> 19.6 us (0.970)
  Pallas kernels: 19.4 us -> 18.8 us
    pallas_call x1, Pallas kernels: 18.8 us -> 18.1 us  [on_device(): pl.pallas_call(section_kernel, out_shape=(pltpu.VMEM((5, *block), F32), p...]
where the time goes in v3:
time: 19.6 us; the launch traced here: 19.4 us
  Pallas kernels  18.8 us (96%)
  between operations  0.64 us (3%)
    pallas_call x1, Pallas kernels, on_device(): pl.pallas_call(section_kernel, out_shape=(pltpu.VMEM((5, *block), F32), p...  18.1 us
    pallas_call x1, Pallas kernels, on_device(): pl.pallas_call(store_kernel, out_shape=(jax.ShapeDtypeStruct(block, F32),...  0.67 us

profile of v3, /device:TPU:1, one launch (start us, length us, event | category | flops | bytes accessed | tf_op | source)
XLA Modules:
  0.0 19.4 jit_solution(15567179360049055899)
XLA Ops:
  0.6 18.1 %shard_map.111 = (f32[5,4,8,128]{3,2,1,0:T(8,128)S(1)}, f32[1,6]{1,0:T(1,128)S(1)}) custom-call(f32[4,8,128]{2,1,0:T(8,128)} %rho_h.1, f32[3,4,8,128]{3,2,1,0:T(8,128)} %mom_h.1, f32[4,8,128]{2,1,0:T(8,128)} %ene_h.1, s32[1,2]{1,0:T(1,128)} %flag_h.1, f32[1,6]{1,0:T(1,128)} %bitcast.2, f32[128,768]{1,0:T(8,128)} %constant.6.clone.radm_h, ...), custom_call_target="tpu_custom_call" | custom-call | tf_op jit(solution)/shard_map/pallas_call | solution.py:704
  18.8 0.7 %shard_map.112 = (f32[4,8,128]{2,1,0:T(8,128)}, f32[3,4,8,128]{3,2,1,0:T(8,128)}, f32[4,8,128]{2,1,0:T(8,128)}, f32[1,6]{1,0:T(1,128)}) custom-call(f32[5,4,8,128]{3,2,1,0:T(8,128)S(1)} %get-tuple-element.10.out_ref, f32[1,6]{1,0:T(1,128)S(1)} %get-tuple-element.11.body_ref), custom_call_target="tpu_custom_call" | custom-call | tf_op jit(solution)/shard_map/pallas_call | solution.py:747

commit v4 on v3

--- a/solution.py
+++ b/solution.py
@@ -171,6 +171,9 @@
     is_teller = is_extra | (is_root & jnp.logical_not(first_column))
     is_far = (ra == 0) & (ax >= 4)
     is_even = lax.rem(az, 2) == 0
+    late = (ax == 0) & (ra == 0)
+    greets_above = (is_even & jnp.logical_not(late & (az == 0))) | (late & (az == AZIM - 1))
+    greets_below = (is_even & jnp.logical_not(late & (az == 0))) | (late & (az == 1))
     on_odd_core = lax.rem(ax, 2) == 1
     column_root = {"axial": ROOT, "radial": 0}
     column_teller = {"axial": jnp.where(first_column, EXTRA, ROOT), "radial": 0}
@@ -235,10 +238,13 @@
 
     below = lax.rem(az + (AZIM - 1), AZIM)
     above = lax.rem(az + 1, AZIM)
-    @pl.when(is_even)
+    @pl.when(greets_above)
+    def _():
+        greet({"azim": above})
+
+    @pl.when(greets_below)
     def _():
         greet({"azim": below})
-        greet({"azim": above})
 
     @pl.when(on_odd_core)
     def _():
@@ -268,8 +274,8 @@
     r = 1.0 + (elem_r + by_place(lane & 3, OFF)) * STEP_R
     r_face = 1.0 + (elem_r + jnp.where(lane == 127, 1.0, 0.0)) * STEP_R
 
-    loads[0].wait()
-    loads[1].wait()
+    for load in loads[:5]:
+        load.wait()
     cos = [ang_s[0, k] for k in range(6)]
     sin = [ang_s[0, 6 + k] for k in range(6)]
     flag = jnp.where(
@@ -286,16 +292,13 @@
         load_w.append(jnp.where(lane < 4, arm * turn, zero))
     load_w = jnp.concatenate(load_w, axis=0)
     wall_a = jnp.where(lane32 < 4, by_place(lane32 & 3, LA), 0.0)
-    loads[2].wait()
-    loads[3].wait()
-    loads[4].wait()
     u = [u_v[f].reshape(32, 128) for f in range(5)]
 
     wall = [jnp.sum(x * wall_a, axis=1, keepdims=True) for x in u]
     own[...] = jnp.sum(pressure_of(wall) * load_w, axis=0, keepdims=True)
 
     by_column = jnp.where(first_column & (ax != EXTRA), 2, 1)
-    greeted = jnp.where(is_even, 0, 2)
+    greeted = jnp.where(greets_above, 0, 1) + jnp.where(greets_below, 0, 1)
     greeted = greeted + jnp.where(on_odd_core, 0, jnp.where(ax > 0, 2, 1))
     greeted = greeted + jnp.where(
         ra == 1, 2, jnp.where(ax == ROOT, AZIM, jnp.where(ax >= 4, AZIM + 1, by_column))
@@ -373,11 +376,14 @@
     azs_lo[5] = mean_a
     azs_hi[5] = mean_a
 
-    def push_azim():
+    def push_below():
         push(azs_lo, azr_hi, 3, {"azim": below}).start()
+
+    def push_above():
         push(azs_hi, azr_lo, 4, {"azim": above}).start()
 
-    pl.when(jnp.logical_not(is_even))(push_azim)
+    pl.when(jnp.logical_not(greets_below))(push_below)
+    pl.when(jnp.logical_not(greets_above))(push_above)
 
     loads[5].wait()
     loads[6].wait()
@@ -422,6 +428,16 @@
         col[...] = own[...] + jnp.sum(p1[...], axis=0)
         p2b[2 * AZIM + az] = col[...]
         tell_all(col, p2b.at[2 * AZIM + az], 8, True)
+
+    @pl.when(greets_below)
+    def _():
+        arrived(azr_lo, 4)
+        push_below()
+
+    @pl.when(greets_above)
+    def _():
+        arrived(azr_hi, 3)
+        push_above()
 
     r32 = jnp.concatenate([r] * 4, axis=0)
     rf32 = jnp.concatenate([r_face] * 4, axis=0)
@@ -447,9 +463,14 @@
         br[f] = k_r * mix_r[160 + 32 * f : 192 + 32 * f]
         bz[f] = k_z * mix_z[:, 640 + 128 * f : 768 + 128 * f]
 
-    arrived(azr_lo, 4)
-    arrived(azr_hi, 3)
-    pl.when(is_even)(push_azim)
+    @pl.when(jnp.logical_not(greets_below))
+    def _():
+        arrived(azr_lo, 4)
+
+    @pl.when(jnp.logical_not(greets_above))
+    def _():
+        arrived(azr_hi, 3)
+
     own_lo = [azs_lo[f] for f in range(6)]
     own_hi = [azs_hi[f] for f in range(6)]
     from_lo = [azr_lo[f] for f in range(6)]
@@ -541,55 +562,36 @@
         br[f] = br[f] + k_r * fix_r[160 + 32 * f : 192 + 32 * f]
         cr[f] = k_r * fix_r[320 + 32 * f : 352 + 32 * f]
 
+    @pl.when(is_root)
+    def _():
+        left(p2b.at[pl.ds(0, AZIM)], 8)
+
+    @pl.when(is_far & (ax >= 6))
+    def _():
+        left(p2b.at[pl.ds(0, AZIM + 1)], 1)
+
+    @pl.when(is_far & (ax < 6))
+    def _():
+        left(p2b.at[pl.ds(0, AZIM + 1)], 8)
+
+    @pl.when(is_near)
+    def _():
+        left(own, 0)
+
+    left(azs_lo, 3)
+    left(azs_hi, 4)
+
+    @pl.when(ax > 0)
+    def _():
+        left(axs, 5)
+
+    @pl.when(ax < AXIAL - 1)
+    def _():
+        left(axs, 6)
+
+    left(rads, 7)
+
     loads[7].wait()
-
-    @pl.when(is_root)
-    def _():
-        arrived(p2b.at[pl.ds(0, 3 * AZIM - 1)], 8)
-
-    @pl.when(is_extra)
-    def _():
-        arrived(p2b, 8)
-
-    @pl.when(is_extra)
-    def _():
-        pl.semaphore_wait(ready_sem, 2 * AXIAL - 2)
-
-    @pl.when(is_teller & is_root)
-    def _():
-        pl.semaphore_wait(ready_sem, 2 * AXIAL - 1)
-
-    def sum_rows(ref, count):
-        sums = [ref[i] for i in range(8)]
-        for i in range(8, count):
-            sums[i % 8] = sums[i % 8] + ref[i]
-        while len(sums) > 1:
-            sums = [x + y for x, y in zip(sums[0::2], sums[1::2])]
-        return sums[0]
-
-    @pl.when(is_root | is_extra)
-    def _():
-        early = sum_rows(p2b, 3 * AZIM)
-        arrived(p2a, 1)
-        p3[...] = early + sum_rows(p2a, 2 * AZIM)
-
-    @pl.when(is_teller)
-    def _():
-        @pl.when(is_root)
-        def _():
-            push(p3, p3, 2, {"axial": EXTRA}).start()
-
-        for k in (2, 0, 4, 5, 6, 7):
-            push(p3, p3, 2, {"axial": k}).start()
-        for k in range(AXIAL):
-            push(p3, p3, 2, {"axial": k, "radial": 1}).start()
-
-    @pl.when(is_told)
-    def _():
-        arrived(p3, 2)
-
-    total = p3[...]
-    load = [jnp.broadcast_to(total[:, i : i + 1], (8, 128)) for i in range(4)]
     v = [body_s[0, i] for i in range(3)]
     om = [body_s[0, 3 + i] for i in range(3)]
     spin = [om[0], om[1], 0.25 * om[2]]
@@ -598,6 +600,55 @@
         om[2] * spin[0] - om[0] * spin[2],
         om[0] * spin[1] - om[1] * spin[0],
     ]
+
+
+    @pl.when(is_root)
+    def _():
+        arrived(p2b.at[pl.ds(0, 3 * AZIM - 1)], 8)
+
+    @pl.when(is_extra)
+    def _():
+        arrived(p2b, 8)
+
+    @pl.when(is_extra)
+    def _():
+        pl.semaphore_wait(ready_sem, 2 * AXIAL - 2)
+
+    @pl.when(is_teller & is_root)
+    def _():
+        pl.semaphore_wait(ready_sem, 2 * AXIAL - 1)
+
+    def sum_rows(ref, count):
+        sums = [ref[i] for i in range(8)]
+        for i in range(8, count):
+            sums[i % 8] = sums[i % 8] + ref[i]
+        while len(sums) > 1:
+            sums = [x + y for x, y in zip(sums[0::2], sums[1::2])]
+        return sums[0]
+
+    @pl.when(is_root | is_extra)
+    def _():
+        early = sum_rows(p2b, 3 * AZIM)
+        arrived(p2a, 1)
+        p3[...] = early + sum_rows(p2a, 2 * AZIM)
+
+    @pl.when(is_teller)
+    def _():
+        @pl.when(is_root)
+        def _():
+            push(p3, p3, 2, {"axial": EXTRA}).start()
+
+        for k in (2, 0, 4, 5, 6, 7):
+            push(p3, p3, 2, {"axial": k}).start()
+        for k in range(AXIAL):
+            push(p3, p3, 2, {"axial": k, "radial": 1}).start()
+
+    @pl.when(is_told)
+    def _():
+        arrived(p3, 2)
+
+    total = p3[...]
+    load = [jnp.broadcast_to(total[:, i : i + 1], (8, 128)) for i in range(4)]
     v0 = v[0] + 60.0 * load[0]
     v1 = v[1] + 60.0 * load[1]
     v2 = jnp.full((8, 128), v[2], F32)
@@ -639,10 +690,6 @@
                 value = value - (d0 * u_v[2, a] - d1 * u_v[1, a])
             out_ref[f, a] = value
 
-    @pl.when(is_root)
-    def _():
-        left(p2b.at[pl.ds(0, AZIM)], 8)
-
     @pl.when(is_teller & is_root)
     def _():
         left(p2b.at[pl.ds(0, 2 * AXIAL - 1)], 2)
@@ -650,31 +697,6 @@
     @pl.when(is_extra)
     def _():
         left(p2b.at[pl.ds(0, 2 * AXIAL - 2)], 2)
-
-    @pl.when(is_far & (ax >= 6))
-    def _():
-        left(p2b.at[pl.ds(0, AZIM + 1)], 1)
-
-    @pl.when(is_far & (ax < 6))
-    def _():
-        left(p2b.at[pl.ds(0, AZIM + 1)], 8)
-
-    @pl.when(is_near)
-    def _():
-        left(own, 0)
-
-    left(azs_lo, 3)
-    left(azs_hi, 4)
-
-    @pl.when(ax > 0)
-    def _():
-        left(axs, 5)
-
-    @pl.when(ax < AXIAL - 1)
-    def _():
-        left(axs, 6)
-
-    left(rads, 7)
 
 
 def store_kernel(out_ref, body_ref, rho_h, mom_h, ene_h, body_h, sems):

time: 19.6 us -> 19.6 us (level)
  no operation moved by 1% of the time
where the time goes in v4:
time: 19.6 us; the launch traced here: 19.4 us
  Pallas kernels  18.8 us (96%)
  between operations  0.64 us (3%)
    pallas_call x1, Pallas kernels, on_device(): pl.pallas_call(section_kernel, out_shape=(pltpu.VMEM((5, *block), F32), p...  18.1 us
    pallas_call x1, Pallas kernels, on_device(): pl.pallas_call(store_kernel, out_shape=(jax.ShapeDtypeStruct(block, F32),...  0.67 us

profile of v4, /device:TPU:1, one launch (start us, length us, event | category | flops | bytes accessed | tf_op | source)
XLA Modules:
  0.0 19.4 jit_solution(14359344398880467257)
XLA Ops:
  0.6 18.1 %shard_map.111 = (f32[5,4,8,128]{3,2,1,0:T(8,128)S(1)}, f32[1,6]{1,0:T(1,128)S(1)}) custom-call(f32[4,8,128]{2,1,0:T(8,128)} %rho_h.1, f32[3,4,8,128]{3,2,1,0:T(8,128)} %mom_h.1, f32[4,8,128]{2,1,0:T(8,128)} %ene_h.1, s32[1,2]{1,0:T(1,128)} %flag_h.1, f32[1,6]{1,0:T(1,128)} %bitcast.2, f32[128,768]{1,0:T(8,128)} %constant.6.clone.radm_h, ...), custom_call_target="tpu_custom_call" | custom-call | tf_op jit(solution)/shard_map/pallas_call | solution.py:726
  18.8 0.7 %shard_map.112 = (f32[4,8,128]{2,1,0:T(8,128)}, f32[3,4,8,128]{3,2,1,0:T(8,128)}, f32[4,8,128]{2,1,0:T(8,128)}, f32[1,6]{1,0:T(1,128)}) custom-call(f32[5,4,8,128]{3,2,1,0:T(8,128)S(1)} %get-tuple-element.10.out_ref, f32[1,6]{1,0:T(1,128)S(1)} %get-tuple-element.11.body_ref), custom_call_target="tpu_custom_call" | custom-call | tf_op jit(solution)/shard_map/pallas_call | solution.py:769

commit v5 on v4

--- a/solution.py
+++ b/solution.py
@@ -160,7 +160,7 @@
     u_v, radm, axm, ang_s, flag_s, body_s,
     own, col, p1, p2a, p2b, p3,
     azs_lo, azs_hi, azr_lo, azr_hi, axs, axr_lo, axr_hi, rads, radr,
-    r0, br, cr, bz, cz, aface,
+    r0, br, cr, bz, cz, by, bo, aface,
     load_sem, send_sem, recv_sem, ready_sem,
 ):
     az, ax, ra = lax.axis_index("azim"), lax.axis_index("axial"), lax.axis_index("radial")
@@ -601,6 +601,37 @@
         om[0] * spin[1] - om[1] * spin[0],
     ]
 
+    o2 = om[2] - 120.0 * gyro[2]
+    swirl = o2 * r
+    for f in range(5):
+        carried = [k_a * u_v[f, k] for k in range(4)]
+        below_mean, above_mean = aface[f], aface[10 + f]
+        for a in range(4):
+            row = slice(8 * a, 8 * a + 8)
+            part = [float(MIX[a, k]) * carried[k] for k in range(4)]
+            part += [float(SC[a]) * below_mean, float(SE[a]) * above_mean]
+            plain = sum(part[1:], part[0])
+            of_x = cos[a] * br[f, row] - sum((sin[k] * part[k] for k in range(1, 6)), sin[0] * part[0])
+            of_y = sin[a] * br[f, row] + sum((cos[k] * part[k] for k in range(1, 6)), cos[0] * part[0])
+            arm = r * bz[f, row]
+            of_o0 = sin[a] * arm - z * of_y
+            of_o1 = z * of_x - cos[a] * arm
+            value = r0[f, row] + swirl * plain + v[2] * bz[f, row]
+            if f == 1:
+                value = value + (DT * o2) * u_v[2, a]
+                of_o1 = of_o1 - DT * u_v[3, a]
+            if f == 2:
+                value = value - (DT * o2) * u_v[1, a]
+                of_o0 = of_o0 + DT * u_v[3, a]
+            if f == 3:
+                of_o0 = of_o0 - DT * u_v[2, a]
+                of_o1 = of_o1 + DT * u_v[1, a]
+            r0[f, row] = value
+            br[f, row] = of_x
+            by[f, row] = of_y
+            bz[f, row] = of_o0
+            bo[f, row] = of_o1
+
 
     @pl.when(is_root)
     def _():
@@ -628,9 +659,9 @@
 
     @pl.when(is_root | is_extra)
     def _():
-        early = sum_rows(p2b, 3 * AZIM)
+        col[...] = sum_rows(p2b, 3 * AZIM)
         arrived(p2a, 1)
-        p3[...] = early + sum_rows(p2a, 2 * AZIM)
+        p3[...] = col[...] + sum_rows(p2a, 2 * AZIM)
 
     @pl.when(is_teller)
     def _():
@@ -651,43 +682,29 @@
     load = [jnp.broadcast_to(total[:, i : i + 1], (8, 128)) for i in range(4)]
     v0 = v[0] + 60.0 * load[0]
     v1 = v[1] + 60.0 * load[1]
-    v2 = jnp.full((8, 128), v[2], F32)
     o0 = om[0] + 30.0 * (load[2] - gyro[0])
     o1 = om[1] + 30.0 * (load[3] - gyro[1])
-    o2 = jnp.full((8, 128), om[2] - 120.0 * gyro[2], F32)
     body_row = zero
-    for i, value in enumerate((v0, v1, v2, o0, o1, o2)):
+    for i, value in enumerate((v0, v1, v[2], o0, o1, o2)):
         body_row = jnp.where(lane == i, value, body_row)
     body_ref[...] = body_row[0:1, 0:6]
 
     along_x = v0 + z * o1
     along_y = v1 - z * o0
-    swirl = o2 * r
 
     def azim_speed(k):
-        return cos[k] * along_y - sin[k] * along_x + swirl
-
-    s_a = [azim_speed(k) for k in range(4)]
+        return jnp.abs(cos[k] * along_y - sin[k] * along_x + swirl)
+
     s_lo, s_hi = azim_speed(4), azim_speed(5)
-    s_r = [cos[a] * along_x + sin[a] * along_y for a in range(4)]
-    s_z = [v2 + r * (o0 * sin[a] - o1 * cos[a]) for a in range(4)]
-    d0, d1, d2 = DT * o0, DT * o1, DT * o2
+    s_r = [jnp.abs(cos[a] * along_x + sin[a] * along_y) for a in range(4)]
+    s_z = [jnp.abs(v[2] + r * (o0 * sin[a] - o1 * cos[a])) for a in range(4)]
     for f in range(5):
-        carried = [k_a * s_a[k] * u_v[f, k] for k in range(4)]
-        at_lo = s_lo * aface[f] + jnp.abs(s_lo) * aface[5 + f]
-        at_hi = s_hi * aface[10 + f] + jnp.abs(s_hi) * aface[15 + f]
+        at_lo, at_hi = s_lo * aface[5 + f], s_hi * aface[15 + f]
         for a in range(4):
             row = slice(8 * a, 8 * a + 8)
-            value = r0[f, row] + s_r[a] * br[f, row] + jnp.abs(s_r[a]) * cr[f, row]
-            value = value + s_z[a] * bz[f, row] + jnp.abs(s_z[a]) * cz[f, row]
-            value = value + weighed(MIX[a], carried)
-            value = value + float(SC[a]) * at_lo + float(SE[a]) * at_hi
-            if f == 1:
-                value = value - (d1 * u_v[3, a] - d2 * u_v[2, a])
-            if f == 2:
-                value = value - (d2 * u_v[1, a] - d0 * u_v[3, a])
-            if f == 3:
-                value = value - (d0 * u_v[2, a] - d1 * u_v[1, a])
+            value = (r0[f, row] + v0 * br[f, row]) + (v1 * by[f, row] + o0 * bz[f, row])
+            value = value + (o1 * bo[f, row] + s_r[a] * cr[f, row])
+            value = value + (s_z[a] * cz[f, row] + float(SC[a]) * at_lo + float(SE[a]) * at_hi)
             out_ref[f, a] = value
 
     @pl.when(is_teller & is_root)
@@ -744,7 +761,7 @@
             *[halo] * 7,
             pltpu.VMEM((32, 128), F32),
             pltpu.VMEM((32, 128), F32),
-            *[part] * 5,
+            *[part] * 7,
             pltpu.VMEM((20, 8, 128), F32),
             pltpu.SemaphoreType.DMA((8,)),
             pltpu.SemaphoreType.DMA((9,)),

time: 19.6 us -> 19.5 us (level)
  no operation moved by 1% of the time
where the time goes in v5:
time: 19.5 us; the launch traced here: 19.4 us
  Pallas kernels  18.8 us (96%)
  between operations  0.64 us (3%)
    pallas_call x1, Pallas kernels, on_device(): pl.pallas_call(section_kernel, out_shape=(pltpu.VMEM((5, *block), F32), p...  18.1 us
    pallas_call x1, Pallas kernels, on_device(): pl.pallas_call(store_kernel, out_shape=(jax.ShapeDtypeStruct(block, F32),...  0.67 us

profile of v5, /device:TPU:1, one launch (start us, length us, event | category | flops | bytes accessed | tf_op | source)
XLA Modules:
  0.0 19.4 jit_solution(14294314115431294624)
XLA Ops:
  0.6 18.1 %shard_map.111 = (f32[5,4,8,128]{3,2,1,0:T(8,128)S(1)}, f32[1,6]{1,0:T(1,128)S(1)}) custom-call(f32[4,8,128]{2,1,0:T(8,128)} %rho_h.1, f32[3,4,8,128]{3,2,1,0:T(8,128)} %mom_h.1, f32[4,8,128]{2,1,0:T(8,128)} %ene_h.1, s32[1,2]{1,0:T(1,128)} %flag_h.1, f32[1,6]{1,0:T(1,128)} %bitcast.2, f32[128,768]{1,0:T(8,128)} %constant.6.clone.radm_h, ...), custom_call_target="tpu_custom_call" | custom-call | tf_op jit(solution)/shard_map/pallas_call | solution.py:743
  18.7 0.7 %shard_map.112 = (f32[4,8,128]{2,1,0:T(8,128)}, f32[3,4,8,128]{3,2,1,0:T(8,128)}, f32[4,8,128]{2,1,0:T(8,128)}, f32[1,6]{1,0:T(1,128)}) custom-call(f32[5,4,8,128]{3,2,1,0:T(8,128)S(1)} %get-tuple-element.10.out_ref, f32[1,6]{1,0:T(1,128)S(1)} %get-tuple-element.11.body_ref), custom_call_target="tpu_custom_call" | custom-call | tf_op jit(solution)/shard_map/pallas_call | solution.py:786
